TPU v7x, 128 devices: a whole 4x4x4 slice. The times are simulated.
128 devices in a mesh: ctx: 4 (over x_lo, core), exp: 32 (over z, x_hi, y).
Axes of the slice: x: 4 (x_hi: 2, x_lo: 2; x = x_hi * 2 + x_lo), y: 4, z: 4, core: 2. Of those that a mesh axis runs over, the one named last changes fastest.
Arguments:
- queries: bfloat16 [16384, 4096], P(('ctx', 'exp')), may hold values from -6 to 6
- fresh_keys: bfloat16 [16384, 256], P(('ctx', 'exp')), may hold values from -6 to 6
- fresh_values: bfloat16 [16384, 256], P(('ctx', 'exp')), may hold values from -6 to 6
- stored_keys: bfloat16 [8192, 256], P('ctx'), may hold values from -6 to 6
- stored_values: bfloat16 [8192, 256], P('ctx'), may hold values from -6 to 6
- column_blocks: int32 [2, 2], replicated, may hold values from 0 to 127, as said below
- diagonal_offsets: int32 [2, 8], replicated, may hold values from 257 to 384
- residual: bfloat16 [16384, 4096], P(('ctx', 'exp')), may hold values from -3 to 3
- norm_gain: float32 [4096], replicated, may hold values from 0.1 to 1.9
- routes: int32 [16384, 8], P(('ctx', 'exp')), may hold values from 0 to 127, all different within a row; in each aligned block of 128 rows (0 to 127, 128 to 255, ...) at most 10 rows name the same one
- gate_weights: float32 [16384, 8], P(('ctx', 'exp')), may hold values from 0.05 to 1
- w_gate: bfloat16 [128, 4096, 768], P(('ctx', 'exp')), may hold values from -0.09375 to 0.09375
- w_up: bfloat16 [128, 4096, 768], P(('ctx', 'exp')), may hold values from -0.09375 to 0.09375
- w_down: bfloat16 [128, 768, 4096], P(('ctx', 'exp')), may hold values from -0.21875 to 0.21875
Outputs:
- mixed: bfloat16 [16384, 4096], P(('ctx', 'exp'))
Inputs may be any that keep to these rules, and one draw needn't show every extreme that they name: `column_blocks`: the vertical blocks of one key-value head differ; the first key-value head reads the last block and the last key-value head reads block 0. `routes`: the 8 experts of a token differ. In each aligned block of 128 tokens (the tokens of one device) no expert is named more than 10 times, a bound that some block reaches.
All inputs are finite; a program needn't handle non-finite values.
Results may differ from a plain program's by a relative error of at most 0.014.
Values may be sent and summed in bfloat16 or wider, within the bound.
A program may use at most 192 MiB of HBM per device.

v0:
```python
import jax
import jax.numpy as jnp
from jax import lax
from jax.sharding import PartitionSpec as P

PATTERN_BLOCK = 64


def candidates(query_block, column_blocks, diagonal_offsets, block_total):
    count = query_block.shape[0]
    heads = column_blocks.shape[0]
    vertical = jnp.broadcast_to(column_blocks[None, :, :], (count, heads, column_blocks.shape[1]))
    slash = query_block[:, None, None] - diagonal_offsets[None, :, :]
    listed = jnp.concatenate([vertical, slash], axis=2)
    width = listed.shape[2]
    inside = (listed >= 0) & (listed < block_total)
    earlier = (
        jnp.arange(width, dtype=jnp.int32)[None, :] < jnp.arange(width, dtype=jnp.int32)[:, None]
    )
    repeated = jnp.any(
        (listed[:, :, :, None] == listed[:, :, None, :]) & earlier[None, None, :, :], axis=-1
    )
    return (listed, inside & jnp.logical_not(repeated))


def body(
    queries,
    fresh_keys,
    fresh_values,
    stored_keys,
    stored_values,
    column_blocks,
    diagonal_offsets,
    residual,
    norm_gain,
    routes,
    gate_weights,
    w_gate,
    w_up,
    w_down,
):
    row_count = queries.shape[0]
    model_width = residual.shape[1]
    heads_kv = column_blocks.shape[0]
    head_dim = fresh_keys.shape[1] // heads_kv
    head_groups = model_width // (heads_kv * head_dim)
    cycle_size = lax.axis_size("ctx")
    expert_axis = lax.axis_size("exp")
    context = stored_keys.shape[0] * cycle_size
    block_total = context // PATTERN_BLOCK
    count_of_queries = row_count // PATTERN_BLOCK
    device_rank = lax.axis_index("ctx") * expert_axis + lax.axis_index("exp")
    query_block = (context + device_rank * row_count) // PATTERN_BLOCK + jnp.arange(
        count_of_queries, dtype=jnp.int32
    )
    listed, usable = candidates(query_block, column_blocks, diagonal_offsets, block_total)
    block_start = jnp.clip(listed, 0, block_total - 1)[..., None] * PATTERN_BLOCK + jnp.arange(
        PATTERN_BLOCK, dtype=jnp.int32
    )
    head_picker = jnp.arange(heads_kv, dtype=jnp.int32)[None, :, None, None]
    score_scale = 1.0 / head_dim**0.5
    query_head_rows = queries.reshape(
        count_of_queries, PATTERN_BLOCK, heads_kv, head_groups, head_dim
    )
    own_score = (
        jnp.einsum(
            "qthgd,qthd->qthg",
            query_head_rows,
            fresh_keys.reshape(count_of_queries, PATTERN_BLOCK, heads_kv, head_dim),
            preferred_element_type=jnp.float32,
        )
        * score_scale
    )
    self_values = fresh_values.reshape(
        count_of_queries, PATTERN_BLOCK, heads_kv, 1, head_dim
    ).astype(jnp.float32)
    denom_sum = jnp.ones_like(own_score)
    weighted = jnp.broadcast_to(
        self_values, (count_of_queries, PATTERN_BLOCK, heads_kv, head_groups, head_dim)
    )
    keys_piece = lax.all_gather(stored_keys, "ctx", axis=0, tiled=True)
    values_piece = lax.all_gather(stored_values, "ctx", axis=0, tiled=True)
    key_count = keys_piece.shape[0]
    key_head_rows = keys_piece.reshape(key_count, heads_kv, head_dim)
    value_head_rows = values_piece.reshape(key_count, heads_kv, head_dim)
    local = block_start
    row_ok = usable[..., None] & (local >= 0) & (local < key_count)
    local = jnp.clip(local, 0, key_count - 1)
    key_rows = key_head_rows[local, head_picker]
    value_rows = value_head_rows[local, head_picker]
    scores = (
        jnp.einsum(
            "qthgd,qhcjd->qthgcj", query_head_rows, key_rows, preferred_element_type=jnp.float32
        )
        * score_scale
    )
    kept = row_ok[:, None, :, None, :, :]
    new_max = jnp.maximum(own_score, jnp.max(jnp.where(kept, scores, -jnp.inf), axis=(-2, -1)))
    weights = jnp.where(kept, jnp.exp(scores - new_max[..., None, None]), 0.0).astype(jnp.bfloat16)
    rescale = jnp.exp(own_score - new_max)
    denom_sum = denom_sum * rescale + jnp.sum(weights, axis=(-2, -1), dtype=jnp.float32)
    weighted = weighted * rescale[..., None] + jnp.einsum(
        "qthgcj,qhcjd->qthgd", weights, value_rows, preferred_element_type=jnp.float32
    )
    _, denom_sum, weighted = (new_max, denom_sum, weighted)
    attended = (weighted / denom_sum[..., None]).reshape(row_count, model_width)
    hidden = residual.astype(jnp.float32) + attended
    spread = jnp.mean(hidden * hidden, axis=-1, keepdims=True)
    normed = (hidden * lax.rsqrt(spread + 1e-06) * norm_gain).astype(jnp.bfloat16)
    experts = cycle_size * expert_axis
    top_count = routes.shape[1]
    capacity = row_count * top_count // experts + row_count * top_count // (4 * experts)
    flat_ids = routes.reshape(-1)
    one_hot = (flat_ids[:, None] == jnp.arange(experts, dtype=jnp.int32)[None, :]).astype(jnp.int32)
    slot_ids = jnp.sum((jnp.cumsum(one_hot, axis=0) - one_hot) * one_hot, axis=1)
    token_ids = jnp.arange(row_count * top_count, dtype=jnp.int32) // top_count
    outgoing = (
        jnp.zeros((experts, capacity, model_width), jnp.bfloat16)
        .at[flat_ids, slot_ids]
        .set(normed[token_ids])
    )
    buffer = lax.all_to_all(outgoing, ("ctx", "exp"), split_axis=0, concat_axis=0, tiled=True)
    buffer_shape = buffer.shape
    rows = buffer.reshape(-1, model_width)
    gate_part = jnp.dot(rows, w_gate[0], preferred_element_type=jnp.float32)
    up_part = jnp.dot(rows, w_up[0], preferred_element_type=jnp.float32)
    act = (jax.nn.silu(gate_part) * up_part).astype(jnp.bfloat16)
    answer = jnp.dot(act, w_down[0], preferred_element_type=jnp.float32).astype(jnp.bfloat16)
    returned = lax.all_to_all(
        answer.reshape(buffer_shape), ("ctx", "exp"), split_axis=0, concat_axis=0, tiled=True
    )
    picked = returned[flat_ids, slot_ids].reshape(row_count, top_count, model_width)
    expert_mix = jnp.sum(picked * gate_weights[:, :, None], axis=1)
    return (hidden + expert_mix).astype(jnp.bfloat16)


def solution(mesh):
    in_specs = (
        P(("ctx", "exp"), None),
        P(("ctx", "exp"), None),
        P(("ctx", "exp"), None),
        P("ctx", None),
        P("ctx", None),
        P(),
        P(),
        P(("ctx", "exp"), None),
        P(),
        P(("ctx", "exp"), None),
        P(("ctx", "exp"), None),
        P(("ctx", "exp"), None, None),
        P(("ctx", "exp"), None, None),
        P(("ctx", "exp"), None, None),
    )
    out_specs = P(("ctx", "exp"), None)
    return jax.shard_map(body, mesh=mesh, in_specs=in_specs, out_specs=out_specs, check_vma=False)
```

profile of v0, /device:TPU:86, one launch (start us, length us, event | category | flops | bytes accessed | tf_op | source)
XLA Modules:
  0.0 791.9 jit_solution(9590740956947554066)
XLA Ops:
  8.0 0.8 copy.59
  9.1 0.7 broadcast_subtract_fusion
  10.8 1.5 copy.77
  12.2 0.9 reshape.288
  16.1 39.7 %all-gather.3.cloned.1.call-done = bf16[8192,256]{1,0:T(8,128)(2,1)} async-done(((bf16[2048,256]{1,0:T(8,128)(2,1)}), bf16[8192,256]{1,0:T(8,128)(2,1)}) %all-gather.3.cloned.1.call-update) | async-done | bytes 4194320 | tf_op jit(solution)/shard_map/all_gather | solution.py:81
  55.8 6.9 reshape.236
  62.8 28.7 %gather_fusion = bf16[2560,128]{1,0:T(8,128)(2,1)S(1)} fusion(bf16[8192,2,128]{2,1,0:T(2,128)(2,1)} %reshape.236, s32[2560]{0:T(1024)S(1)} %reshape.249), kind=kCustom, calls=%fused_computation | custom fusion | bytes 1331200 | tf_op jit(solution)/shard_map/gather | solution.py:89
  91.4 4.5 fusion
  96.0 5.8 convert_reduce_fusion
  101.8 1.1 copy-done
  103.0 2.0 all-gather.5.cloned.1.call-done
  104.9 6.9 reshape.237
  111.9 28.1 %gather_fusion.1 = bf16[2560,128]{1,0:T(8,128)(2,1)S(1)} fusion(bf16[8192,2,128]{2,1,0:T(2,128)(2,1)} %reshape.237, s32[2560]{0:T(1024)S(1)} %reshape.249), kind=kCustom, calls=%fused_computation.1 | custom fusion | bytes 1331200 | tf_op jit(solution)/shard_map/gather | solution.py:90
  140.0 9.7 %fusion.18 = f32[2,64,2,16,128]{4,1,3,2,0:T(8,128)S(1)} fusion(bf16[2,2,10,64,128,1]{4,3,5,2,1,0:T(8,128)(2,1)S(1)} %bitcast.98, f32[2,64,2,16]{1,3,2,0:T(8,128)S(1)} %get-tuple-element.5, f32[2,64,2,16]{1,3,2,0:T(8,128)S(1)} %get-tuple-element.6, f32[2,64,2,128]{3,1,2,0:T(8,128)S(1)} %copy.55, f32[2,2,10,64,64,16]{4,3,5,2,1,0:T(8,128)} %copy-done, ...), kind=kOutput, calls=%fused_computation.25 | convolution fusion | flops 683147264 | bytes 13421056 | tf_op jit(solution)/shard_map/qthgcj,qhcjd->qthgd/dot_general | solution.py:102
  149.8 2.6 copy.58
  152.4 1.7 reshape.238
  154.5 1.9 multiply_convert_fusion
  156.4 7.8 gather_fusion.2
  164.2 19.1 %scatter_custom_fusion = bf16[1280,4096]{1,0:T(8,128)(2,1)} fusion(s32[1024]{0:T(1024)S(1)} %broadcast_select_fusion, bf16[1024,4096]{1,0:T(8,128)(2,1)} %gather_fusion.2, bf16[]{:T(256)} %constant.80.clone.1), kind=kCustom, calls=%fused_computation.20 | custom fusion | bytes 10486272
  183.3 11.4 %copy.64 = bf16[128,10,4096]{2,1,0:T(8,128)(2,1)S(1)} copy(bf16[128,10,4096]{2,0,1:T(8,128)(2,1)} %bitcast.93) | data formatting | bytes 20971520 | tf_op jit(solution)/shard_map/scatter | solution.py:120
  194.7 202.8 %all_to_all.10 = bf16[128,10,4096]{2,1,0:T(8,128)(2,1)} all-to-all(bf16[128,10,4096]{2,1,0:T(8,128)(2,1)S(1)} %copy.64), channel_id=1, replica_groups=mesh['ctx'=4,'exp'=32] {'ctx','exp'}, dimensions={0} | all-to-all | bytes 20971520 | tf_op jit(solution)/shard_map/all_to_all | solution.py:122
  397.5 16.7 %reshape.241 = bf16[1280,4096]{1,0:T(8,128)(2,1)} reshape(bf16[128,10,4096]{2,1,0:T(8,128)(2,1)} %all_to_all.10) | data formatting | bytes 20971520 | tf_op jit(solution)/shard_map/reshape | solution.py:124
  414.2 12.3 %fusion.8 = f32[1280,768]{1,0:T(8,128)S(1)} fusion(bf16[1280,4096]{1,0:T(8,128)(2,1)} %reshape.241, bf16[1,4096,768]{2,1,0:T(8,128)(2,1)} %param.25), kind=kOutput, calls=%fused_computation.18 | convolution fusion | flops 8053063680 | bytes 20709376 | tf_op jit(solution)/shard_map/dot_general | solution.py:125
  426.5 9.0 %fusion.15 = bf16[1280,768]{1,0:T(8,128)(2,1)S(1)} fusion(bf16[1280,4096]{1,0:T(8,128)(2,1)S(1)} %copy-done.4, bf16[1,4096,768]{2,1,0:T(8,128)(2,1)S(1)} %bitcast.102, f32[1280,768]{1,0:T(8,128)S(1)} %fusion.8), kind=kOutput, calls=%fused_computation.23 | convolution fusion | flops 8058961920 | bytes 22675456 | tf_op jit(solution)/shard_map/dot_general | solution.py:126
  435.5 13.5 %convolution_convert_fusion = bf16[1280,4096]{1,0:T(8,128)(2,1)} fusion(bf16[1280,768]{1,0:T(8,128)(2,1)S(1)} %fusion.15, bf16[1,768,4096]{2,1,0:T(8,128)(2,1)} %param.27), kind=kOutput, calls=%fused_computation.14 | convolution fusion | flops 8058306560 | bytes 18743296 | tf_op jit(solution)/shard_map/dot_general | solution.py:128
  449.0 15.2 %reshape.242 = bf16[128,10,4096]{2,1,0:T(8,128)(2,1)} reshape(bf16[1280,4096]{1,0:T(8,128)(2,1)} %convolution_convert_fusion) | data formatting | bytes 20971520 | tf_op jit(solution)/shard_map/reshape | solution.py:130
  464.2 13.5 %all-to-all-start.1 = ((bf16[128,10,4096]{2,1,0:T(8,128)(2,1)}), bf16[128,10,4096]{2,1,0:T(8,128)(2,1)}, u32[]{:S(2)}, u32[]{:S(2)}) async-start(bf16[128,10,4096]{2,1,0:T(8,128)(2,1)} %reshape.242), calls=%async_computation.1 | async-start | bytes 33554432 | tf_op jit(solution)/shard_map/all_to_all | solution.py:129
  477.8 244.3 %all-to-all-done.1 = bf16[128,10,4096]{2,1,0:T(8,128)(2,1)} async-done(((bf16[128,10,4096]{2,1,0:T(8,128)(2,1)}), bf16[128,10,4096]{2,1,0:T(8,128)(2,1)}, u32[]{:S(2)}, u32[]{:S(2)}) %all-to-all-start.1) | async-done | bytes 10485792 | tf_op jit(solution)/shard_map/all_to_all | solution.py:129
  722.2 12.1 %copy.65 = bf16[128,10,4096]{2,0,1:T(8,128)(2,1)} copy(bf16[128,10,4096]{2,1,0:T(8,128)(2,1)} %all-to-all-done.1) | data formatting | bytes 20971520 | tf_op jit(solution)/shard_map/all_to_all | solution.py:129
  734.3 34.1 %gather_fusion.3 = bf16[1024,4096]{1,0:T(8,128)(2,1)} fusion(bf16[128,10,4096]{2,0,1:T(8,128)(2,1)} %copy.65, s32[1024]{0:T(1024)S(1)} %bitcast.92), kind=kCustom, calls=%fused_computation.3 | custom fusion | bytes 16785408 | tf_op jit(solution)/shard_map/gather | solution.py:132
  768.4 13.4 %fusion.4 = f32[128,4096]{1,0:T(8,128)} fusion(bf16[1024,4096]{1,0:T(8,128)(2,1)} %gather_fusion.3, f32[128,8]{1,0:T(8,128)S(1)} %copy.66), kind=kLoop, calls=%fused_computation.13 | loop fusion | flops 12058624 | bytes 10489856 | tf_op jit(solution)/shard_map/reduce_sum | solution.py:133
  781.8 2.9 add_convert_fusion
  (67 shorter events, 6.1 us)
Async XLA Ops:
  6.5 8.9 %copy-start.11 = (s32[2]{0:T(128)S(1)}, s32[2]{0:T(128)}, u32[]{:S(2)}) copy-start(s32[2]{0:T(128)} %constant.90) | copy-start | bytes 28
  6.5 9.0 %copy-start.10 = (s32[2]{0:T(128)S(1)}, s32[2]{0:T(128)}, u32[]{:S(2)}) copy-start(s32[2]{0:T(128)} %constant.93) | copy-start | bytes 28
  6.5 7.3 copy-start.7
  6.5 49.3 %all-gather.3.cloned.1.call-start = ((), (), s32[]{:S(2)}) async-start(), calls=%async_computation.2 | async-start | bytes 5242880 | tf_op jit(solution)/shard_map/all_gather | solution.py:81
  7.3 97.7 %all-gather.5.cloned.1.call-start = ((), (), s32[]{:S(2)}) async-start(), calls=%async_computation.3 | async-start | bytes 5242880 | tf_op jit(solution)/shard_map/all_gather | solution.py:82
  96.0 7.0 copy-start
  149.8 4.3 copy-start.5
  149.8 4.7 copy-start.8
  154.1 10.1 %copy-start.2 = (f32[128,4096]{1,0:T(8,128)}, f32[128,4096]{1,0:T(8,128)S(1)}, u32[]{:S(2)}) copy-start(f32[128,4096]{1,0:T(8,128)S(1)} %reshape.238) | copy-start | bytes 6291460
  397.5 29.0 %slice-start = ((s8[6291456]{0:T(1024)(128)(4,1)}), s8[2097152]{0:T(1024)(128)(4,1)S(1)}, s32[]{:S(2)}) async-start(s8[6291456]{0:T(1024)(128)(4,1)} %bitcast.101), calls=%async_computation.4 | async-start | bytes 4194304
  414.2 12.3 %copy-start.4 = (bf16[1280,4096]{1,0:T(8,128)(2,1)S(1)}, bf16[1280,4096]{1,0:T(8,128)(2,1)}, u32[]{:S(2)}) copy-start(bf16[1280,4096]{1,0:T(8,128)(2,1)} %reshape.241) | copy-start | bytes 31457284
  414.2 12.3 %slice-start.1 = ((s8[6291456]{0:T(1024)(128)(4,1)}), s8[4194304]{0:T(1024)(128)(4,1)S(1)}, s32[]{:S(2)}) async-start(s8[6291456]{0:T(1024)(128)(4,1)} %bitcast.101), calls=%async_computation.5 | async-start | bytes 8388608
  464.2 13.5 %copy-start.9 = (f32[128,8]{0,1:T(8,128)S(1)}, f32[128,8]{0,1:T(8,128)}, u32[]{:S(2)}) copy-start(f32[128,8]{0,1:T(8,128)} %param.24) | copy-start | bytes 12292
  464.2 258.0 %all-to-all-start.1 = ((bf16[128,10,4096]{2,1,0:T(8,128)(2,1)}), bf16[128,10,4096]{2,1,0:T(8,128)(2,1)}, u32[]{:S(2)}, u32[]{:S(2)}) async-start(bf16[128,10,4096]{2,1,0:T(8,128)(2,1)} %reshape.242), calls=%async_computation.1 | async-start | bytes 33554432 | tf_op jit(solution)/shard_map/all_to_all | solution.py:129
  477.8 256.5 %copy-start.1 = (s32[1024,1]{0,1:T(1,128)S(1)}, s32[1024,1]{0,1:T(1,128)}, u32[]{:S(2)}) copy-start(s32[1024,1]{0,1:T(1,128)} %get-tuple-element.7) | copy-start | bytes 12292
  768.4 13.4 %copy-start.3 = (f32[128,4096]{1,0:T(8,128)S(1)}, f32[128,4096]{1,0:T(8,128)}, u32[]{:S(2)}) copy-start(f32[128,4096]{1,0:T(8,128)} %copy-done.2) | copy-start | bytes 6291460
  768.4 13.4 %copy-start.6 = (bf16[128,4096]{1,0:T(8,128)(2,1)S(1)}, bf16[128,4096]{1,0:T(8,128)(2,1)}, u32[]{:S(2)}) copy-start(bf16[128,4096]{1,0:T(8,128)(2,1)} %param.21) | copy-start | bytes 3145732
Sparse Core Ops, SparseCore 0:
  9.0 46.7 all-gather.2
  57.5 47.3 all-gather.4
where the time goes:
time: 803 us; the launch traced here: 792 us
  waiting for transfers between devices  287 us (36%)
  blocking collectives  203 us (25%)
  local copies, waits for them, and re-layouts  197 us (25%)
  matrix products  49.7 us (6%)
  other arithmetic  27.1 us (3%)
  between operations  14.1 us (2%)
  starting transfers between devices  13.6 us (2%)
    all_to_all x1, waiting for transfers between devices, body(): lax.all_to_all(answer.reshape(buffer_shape), ('ctx', 'exp'), split_axis=0...  244 us
    all_to_all x1, blocking collectives, body(): lax.all_to_all(outgoing, ('ctx', 'exp'), split_axis=0, concat_axis=0, til...  203 us
    all_gather x1, waiting for transfers between devices, body(): keys_piece = lax.all_gather(stored_keys, 'ctx', axis=0, tiled=True)  39.7 us
    gather x1, local copies, waits for them, and re-layouts, body(): returned[flat_ids, slot_ids].reshape(row_count, top_count, model_width)  34.1 us
    gather x1, local copies, waits for them, and re-layouts, body(): key_rows = key_head_rows[local, head_picker]  28.7 us
    gather x1, local copies, waits for them, and re-layouts, body(): value_rows = value_head_rows[local, head_picker]  28.1 us
    unnamed x32, local copies, waits for them, and re-layouts  22.6 us
    reshape x1, local copies, waits for them, and re-layouts, body(): rows = buffer.reshape(-1, model_width)  16.7 us
  transfers between devices with their start and end apart: 3, of which 3 were waited for; matrix products, arithmetic and copies ran while one was open for 7% of the time, Pallas kernels for 0%

commit v1 on v0

v1 whole, which is shorter than its diff:
```python
import functools

import jax
import jax.numpy as jnp
from jax import lax
from jax.experimental import pallas as pl
from jax.experimental.pallas import tpu as pltpu
from jax.sharding import PartitionSpec as P

MESH = pl.DeviceIdType.MESH
BF16 = jnp.bfloat16
F32 = jnp.float32
BLOCK = 64
HEAD = 128
HEADS_KV = 2
GROUP = 16
VERT = 2
SLASH = 8
SLOTS = VERT + 2 * SLASH
TOK = 128
D = 4096
FF = 768
HALF = D // 2
CAP = 10
PLANE = 32
MSG = 8 * CAP
ROWS = 16 * MSG
ALL = PLANE * MSG
PIECE = 256
PIECES = HALF // PIECE
NEG = -1e30


def coords():
    ctx = lax.axis_index("ctx")
    exp = lax.axis_index("exp")
    return ((exp // 4) % 2) * 2 + ctx // 2, exp % 4, exp // 8, ctx % 2


def device(x, y, z, c):
    return ((x % 2) * 2 + c, z * 8 + (x // 2) * 4 + y)


def plane_index(x, y, c):
    return ((x % 2) * 2 + c) * 8 + (x // 2) * 4 + y


def ordered_offsets():
    left = [(dx, dy, dc) for dx in range(4) for dy in range(4) for dc in range(2) if dx or dy or dc]
    use = {}
    out = []

    def links(o):
        found = []
        for axis in range(2):
            if o[axis] == 1:
                found.append((axis, 1))
            elif o[axis] == 3:
                found.append((axis, -1))
            elif o[axis] == 2:
                found += [(axis, 1), (axis, -1)]
        return found

    while left:
        best = min(left, key=lambda o: (sum(2 * use.get(k, 0) + 1 for k in links(o)), -len(links(o)), o))
        left.remove(best)
        out.append(best)
        for k in links(best):
            use[k] = use.get(k, 0) + 1
    return out


OFFSETS = ordered_offsets()
COLUMN = [(1, 0), (3, 1), (2, 0), (3, 0), (1, 1), (2, 1), (0, 1)]


def to_plane(o):
    x, y, z, c = coords()
    return (x + o[0]) % 4, (y + o[1]) % 4, z, (c + o[2]) % 2


def from_plane(o):
    x, y, z, c = coords()
    return (x + 4 - o[0]) % 4, (y + 4 - o[1]) % 4, z, (c + 2 - o[2]) % 2


def to_column(o):
    x, y, z, c = coords()
    return x, y, (z + o[0]) % 4, (c + o[1]) % 2


def from_column(o):
    x, y, z, c = coords()
    return x, y, (z + 4 - o[0]) % 4, (c + 2 - o[1]) % 2


def greet_all():
    bar = pltpu.get_barrier_semaphore()
    for o in OFFSETS:
        pl.semaphore_signal(bar, inc=1, device_id=device(*to_plane(o)), device_id_type=MESH)
    for o in COLUMN[:-1]:
        pl.semaphore_signal(bar, inc=1, device_id=device(*to_column(o)), device_id_type=MESH)
    pl.semaphore_wait(bar, len(OFFSETS) + len(COLUMN) - 1)


def collect_kernel(cols, offs, keys, values, con, near):
    ctx = lax.axis_index("ctx")
    exp = lax.axis_index("exp")
    xl = ctx // 2

    def put(h, slot, block_a, block_b):
        near_a = block_a - 32 * ctx
        near_b = block_b - 32 * ctx
        local = jnp.where((near_a >= 0) & (near_a < 32), near_a, near_b)
        inside = (local >= 0) & (local < 32)
        start = pl.multiple_of(jnp.clip(local, 0, 31) * BLOCK, BLOCK)
        factor = jnp.where(inside, 1.0, 0.0).astype(BF16)
        for kind, ref in ((0, keys), (1, values)):
            block = ref[pl.ds(start, BLOCK), h * HEAD : (h + 1) * HEAD]
            con[kind, h, slot * BLOCK : (slot + 1) * BLOCK, :] = block * factor

    for h in range(HEADS_KV):
        for v in range(VERT):
            put(h, v, cols[h, v], cols[h, v])
            here = (cols[h, v] // 64) == xl
            near[h * SLOTS + v] = jnp.full((8, HEAD), jnp.where(here, 1.0, 0.0), F32)
        for i in range(2):
            for s in range(SLASH):
                block_2 = 256 + 2 * exp + i - offs[h, s]
                slot = VERT + i * SLASH + s
                put(h, slot, block_2, block_2 + 64)
                near[h * SLOTS + slot] = jnp.full((8, HEAD), jnp.where(block_2 >= 0, 1.0, 0.0), F32)


def collect(cols, offs, keys, values):
    return pl.pallas_call(
        collect_kernel,
        name="collect_blocks",
        out_shape=[
            jax.ShapeDtypeStruct((2, HEADS_KV, SLOTS * BLOCK, HEAD), BF16),
            jax.ShapeDtypeStruct((HEADS_KV * SLOTS, 8, HEAD), F32),
        ],
        in_specs=[pl.BlockSpec(memory_space=pltpu.SMEM)] * 2 + [pl.BlockSpec(memory_space=pltpu.VMEM)] * 2,
        out_specs=[pl.BlockSpec(memory_space=pltpu.VMEM)] * 2,
        compiler_params=pltpu.CompilerParams(vmem_limit_bytes=16 * 2**20),
    )(cols, offs, keys, values)


def exchange_kernel(con, near, out, sib, chip, rem, fin, arr, ssem, rsem):
    x, y, z, c = coords()
    xl = x % 2
    exp = lax.axis_index("exp")
    twin = (xl * 2 + 1 - c, exp)
    across = ((1 - xl) * 2 + c, exp)
    bar = pltpu.get_barrier_semaphore()
    for other in (twin, across):
        pl.semaphore_signal(bar, inc=1, device_id=other, device_id_type=MESH)
    pl.semaphore_wait(bar, 2)

    first = pltpu.make_async_remote_copy(
        src_ref=con.at[1 - c], dst_ref=sib, send_sem=ssem.at[0], recv_sem=rsem.at[0],
        device_id=twin, device_id_type=MESH,
    )
    first.start()
    first.wait()
    chip[...] = con[c] + sib[...]

    verts = VERT * BLOCK

    def whole(h):
        return pltpu.make_async_remote_copy(
            src_ref=chip.at[h], dst_ref=rem.at[h], send_sem=ssem.at[1 + h], recv_sem=rsem.at[1 + h],
            device_id=across, device_id_type=MESH,
        )

    def vertical(h):
        return pltpu.make_async_remote_copy(
            src_ref=chip.at[h, pl.ds(0, verts)], dst_ref=rem.at[h, pl.ds(0, verts)],
            send_sem=ssem.at[1 + h], recv_sem=rsem.at[1 + h],
            device_id=across, device_id_type=MESH,
        )

    @pl.when(xl == 0)
    def _():
        for h in range(HEADS_KV):
            whole(h).start()

    @pl.when(xl == 1)
    def _():
        for h in range(HEADS_KV):
            vertical(h).start()

    def back(h):
        return pltpu.make_async_remote_copy(
            src_ref=fin.at[h], dst_ref=arr.at[h], send_sem=ssem.at[3 + h], recv_sem=rsem.at[3 + h],
            device_id=twin, device_id_type=MESH,
        )

    def pick(h, slot):
        span = slice(slot * BLOCK, (slot + 1) * BLOCK)
        local = near[h * SLOTS + slot, 0:1, :].astype(BF16)
        far = rem[h, span, :]
        return span, chip[h, span, :] * local + far * (1.0 - local).astype(BF16), far

    def pick_verticals(h):
        for v in range(VERT):
            span, mixed, _ = pick(h, v)
            fin[h, span, :] = mixed
            out[c, h, span, :] = mixed

    for h in range(HEADS_KV):

        @pl.when(xl == 0)
        def _():
            vertical(h).wait_recv()
            pick_verticals(h)
            fin[h, verts:, :] = jnp.zeros((2 * SLASH * BLOCK, HEAD), BF16)
            out[c, h, verts:, :] = jnp.zeros((2 * SLASH * BLOCK, HEAD), BF16)

        @pl.when(xl == 1)
        def _():
            whole(h).wait_recv()
            pick_verticals(h)
            for slot in range(VERT, SLOTS):
                span, mixed, far = pick(h, slot)

                @pl.when(c == 1)
                def _():
                    out[1, h, span, :] = mixed
                    fin[h, span, :] = far

                @pl.when(c == 0)
                def _():
                    out[0, h, span, :] = far
                    fin[h, span, :] = mixed

        back(h).start()

    for h in range(HEADS_KV):
        back(h).wait()
        out[1 - c, h] = arr[h]

    @pl.when(xl == 0)
    def _():
        for h in range(HEADS_KV):
            whole(h).wait_send()

    @pl.when(xl == 1)
    def _():
        for h in range(HEADS_KV):
            vertical(h).wait_send()


def exchange(con, near):
    part = (HEADS_KV, SLOTS * BLOCK, HEAD)
    return pl.pallas_call(
        exchange_kernel,
        name="key_exchange",
        out_shape=jax.ShapeDtypeStruct((2,) + part, BF16),
        in_specs=[pl.BlockSpec(memory_space=pltpu.VMEM)] * 2,
        out_specs=pl.BlockSpec(memory_space=pltpu.VMEM),
        scratch_shapes=[
            pltpu.VMEM(part, BF16),
            pltpu.VMEM(part, BF16),
            pltpu.VMEM(part, BF16),
            pltpu.VMEM(part, BF16),
            pltpu.VMEM(part, BF16),
            pltpu.SemaphoreType.DMA((5,)),
            pltpu.SemaphoreType.DMA((5,)),
        ],
        compiler_params=pltpu.CompilerParams(
            collective_id=1, has_side_effects=True, vmem_limit_bytes=24 * 2**20
        ),
    )(con, near)


def attend_kernel(cols, offs, q, fk, fv, kv, res, gain, routes, gates, hidden, normed, code, weight):
    ctx = lax.axis_index("ctx")
    exp = lax.axis_index("exp")
    scale = 1.0 / HEAD**0.5
    lane = lax.broadcasted_iota(jnp.int32, (1, (VERT + SLASH) * BLOCK), 1) // BLOCK
    heads = 4
    ones = jnp.ones(((VERT + SLASH) * BLOCK, HEAD), BF16)
    for h in range(HEADS_KV):
        for i in range(2):
            block = 128 + 2 * (ctx * 32 + exp) + i
            listed = [cols[h, v] for v in range(VERT)] + [block - offs[h, s] for s in range(SLASH)]
            bias = jnp.zeros(lane.shape, F32)
            for n, one in enumerate(listed):
                kept = (one >= 0) & (one < 128)
                for before in listed[:n]:
                    kept = kept & (one != before)
                bias = jnp.where(lane == n, jnp.where(kept, 0.0, NEG), bias)
            slash = VERT * BLOCK + i * SLASH * BLOCK
            k = jnp.concatenate([kv[0, h, : VERT * BLOCK, :], kv[0, h, slash : slash + SLASH * BLOCK, :]], axis=0)
            v = jnp.concatenate([kv[1, h, : VERT * BLOCK, :], kv[1, h, slash : slash + SLASH * BLOCK, :]], axis=0)
            v = jnp.concatenate([v, ones], axis=1)
            rows = slice(i * BLOCK, (i + 1) * BLOCK)
            own_k = fk[rows, h * HEAD : (h + 1) * HEAD].astype(F32)
            own_v = fv[rows, h * HEAD : (h + 1) * HEAD].astype(F32)
            own_k = jnp.concatenate([own_k] * heads, axis=0)
            own_v = jnp.concatenate([own_v] * heads, axis=0)
            for g in range(0, GROUP, heads):
                spans = [slice((h * GROUP + g + n) * HEAD, (h * GROUP + g + n + 1) * HEAD) for n in range(heads)]
                part = jnp.concatenate([q[rows, span] for span in spans], axis=0)
                scores = lax.dot_general(part, k, (((1,), (1,)), ((), ())), preferred_element_type=F32)
                scores = scores * scale + bias
                own = jnp.sum(part.astype(F32) * own_k, axis=1, keepdims=True) * scale
                top = jnp.maximum(own, jnp.max(scores, axis=1, keepdims=True))
                weights = jnp.exp(scores - top).astype(BF16)
                own_weight = jnp.exp(own - top).astype(BF16).astype(F32)
                both = jnp.dot(weights, v, preferred_element_type=F32)
                numer = both[:, :HEAD] + own_weight * own_v
                denom = both[:, HEAD:] + own_weight
                attended = numer / denom
                for n, span in enumerate(spans):
                    hidden[rows, span] = res[rows, span].astype(F32) + attended[n * BLOCK : (n + 1) * BLOCK]

    for r in range(0, TOK, 16):
        part = hidden[r : r + 16, :]
        spread = jnp.mean(part * part, axis=1, keepdims=True)
        normed[r : r + 16, :] = (part * lax.rsqrt(spread + 1e-6) * gain[...]).astype(BF16)

    ids = routes[...]
    ids = ((ids // 8) % 4) * 32 + (ids // 32) * 8 + ids % 8
    lanes = lax.broadcasted_iota(jnp.int32, (TOK, TOK), 1)
    named = jnp.zeros((TOK, TOK), F32)
    strength = jnp.zeros((TOK, TOK), F32)
    for n in range(8):
        hit = ids[:, n : n + 1] == lanes
        named = named + jnp.where(hit, 1.0, 0.0)
        strength = strength + jnp.where(hit, gates[:, n : n + 1], 0.0)
    earlier = (lanes < lax.broadcasted_iota(jnp.int32, (TOK, TOK), 0)).astype(BF16)
    place = jnp.dot(earlier, named.astype(BF16), preferred_element_type=F32)
    code[...] = jnp.where(named > 0.5, place, -1.0).T.astype(BF16)
    weight[...] = strength.T.astype(BF16)


def attend(cols, offs, q, fk, fv, kv, res, gain, routes, gates):
    return pl.pallas_call(
        attend_kernel,
        name="attention",
        out_shape=[
            jax.ShapeDtypeStruct((TOK, D), F32),
            jax.ShapeDtypeStruct((TOK, D), BF16),
            jax.ShapeDtypeStruct((TOK, TOK), BF16),
            jax.ShapeDtypeStruct((TOK, TOK), BF16),
        ],
        in_specs=[pl.BlockSpec(memory_space=pltpu.SMEM)] * 2 + [pl.BlockSpec(memory_space=pltpu.VMEM)] * 8,
        out_specs=[pl.BlockSpec(memory_space=pltpu.VMEM)] * 4,
        compiler_params=pltpu.CompilerParams(vmem_limit_bytes=32 * 2**20),
    )(cols, offs, q, fk, fv, kv, res, gain.reshape(1, D), routes, gates)


def table_rows():
    row = lax.broadcasted_iota(jnp.int32, (MSG, TOK), 0)
    block = jnp.zeros((MSG, TOK), jnp.int32)
    for b in range(1, 8):
        block = block + jnp.where(row >= b * CAP, 1, 0)
    return block, (row - block * CAP).astype(F32)


def dispatch_kernel(
    normed, code, weight, w_gate, w_up, act, codes_out, weights_out,
    x_all, codes, weights, select, stage, got, wg, wu, acc,
    wsem, tab_s, tab_r, col_s, col_r, msg_s, msg_r,
):
    x, y, z, c = coords()
    loads = [
        pltpu.make_async_copy(w_gate, wg, wsem.at[0]),
        pltpu.make_async_copy(w_up, wu, wsem.at[1]),
    ]
    for load in loads:
        load.start()
    greet_all()
    me = z * 2 + c

    def tables(n, o, dev, slot):
        return [
            pltpu.make_async_remote_copy(
                src_ref=src.at[dev[2]], dst_ref=dst.at[slot], send_sem=tab_s.at[t, n], recv_sem=tab_r.at[t, n],
                device_id=device(*dev), device_id_type=MESH,
            )
            for t, (src, dst) in enumerate(((code, codes), (weight, weights)))
        ]

    def column_copy(n, j, dev, slot):
        start = pl.multiple_of(dev[3] * HALF + j * PIECE, PIECE)
        return pltpu.make_async_remote_copy(
            src_ref=normed.at[:, pl.ds(start, PIECE)],
            dst_ref=x_all.at[j, pl.ds(pl.multiple_of(slot * TOK, TOK), TOK)],
            send_sem=col_s.at[j, n], recv_sem=col_r.at[j, n],
            device_id=device(*dev), device_id_type=MESH,
        )

    for n, o in enumerate(COLUMN):
        for one in tables(n, o, to_column(o), me):
            one.start()

    def send_columns(j, carry):
        for n, o in enumerate(COLUMN):
            column_copy(n, j, to_column(o), me).start()
        return carry

    lax.fori_loop(0, PIECES, send_columns, 0)

    mine = pl.ds(pl.multiple_of(me * TOK, TOK), TOK)
    for j in range(PIECES):
        start = pl.multiple_of(c * HALF + j * PIECE, PIECE)
        x_all[j, mine, :] = normed[:, pl.ds(start, PIECE)]
    codes[me] = code[z]
    weights[me] = weight[z]
    acc[...] = jnp.zeros_like(acc)

    for n, o in enumerate(COLUMN):
        dev = from_column(o)
        for one in tables(n, o, dev, dev[2] * 2 + dev[3]):
            one.wait()

    block, place = table_rows()
    codes_out[...] = codes[...].astype(F32)
    weights_out[...] = weights[...].astype(F32)

    def fill(l, carry):
        for b in range(8):
            row = codes_out[b, pl.ds(l, 1), :]
            hit = (row == place) & (block == b)
            select[pl.ds(pl.multiple_of(l * MSG, 16), MSG), b * TOK : (b + 1) * TOK] = jnp.where(hit, 1.0, 0.0).astype(BF16)
        return carry

    lax.fori_loop(0, PLANE, fill, 0)

    def message(k, j, dev, src_dev):
        to = plane_index(dev[0], dev[1], dev[3])
        chip = src_dev[0] * 4 + src_dev[1]
        return pltpu.make_async_remote_copy(
            src_ref=stage.at[j % 2, pl.ds(pl.multiple_of(to * MSG, 16), MSG)],
            dst_ref=got.at[j, src_dev[3], pl.ds(pl.multiple_of(chip * MSG, 16), MSG)],
            send_sem=msg_s.at[j, k], recv_sem=msg_r.at[j, k],
            device_id=device(*dev), device_id_type=MESH,
        )

    here = (x, y, z, c)
    own_rows = pl.ds(pl.multiple_of(plane_index(x, y, c) * MSG, 16), MSG)
    own_place = pl.ds(pl.multiple_of((x * 4 + y) * MSG, 16), MSG)

    def send_piece(j):
        for n, o in enumerate(COLUMN):
            dev = from_column(o)
            column_copy(n, j, dev, dev[2] * 2 + dev[3]).wait_recv()

        @pl.when(j >= 2)
        def _():
            for k, o in enumerate(OFFSETS):
                message(k, j - 2, to_plane(o), here).wait_send()

        step = ALL // 8

        def tile(t, carry):
            rows = pl.ds(pl.multiple_of(t * step, 16), step)
            stage[j % 2, rows, :] = jnp.dot(select[rows, :], x_all[j], preferred_element_type=F32).astype(BF16)
            return carry

        lax.fori_loop(0, 8, tile, 0)
        for k, o in enumerate(OFFSETS):
            message(k, j, to_plane(o), here).start()
        got[j, c, own_place, :] = stage[j % 2, own_rows, :]

    def use_piece(j):
        for k, o in enumerate(OFFSETS):
            message(k, j, here, from_plane(o)).wait_recv()
        low = pl.ds(pl.multiple_of(j * PIECE, PIECE), PIECE)
        high = pl.ds(pl.multiple_of(HALF + j * PIECE, PIECE), PIECE)
        step = ROWS // 5

        def tile(t, carry):
            rows = pl.ds(pl.multiple_of(t * step, 16), step)
            left = got[j, 0, rows, :]
            right = got[j, 1, rows, :]
            for n, w in enumerate((wg, wu)):
                acc[n, rows, :] += jnp.dot(left, w[low, :], preferred_element_type=F32) + jnp.dot(
                    right, w[high, :], preferred_element_type=F32
                )
            return carry

        lax.fori_loop(0, 5, tile, 0)

    def step(j, carry):
        @pl.when(j < PIECES)
        def _():
            send_piece(j)

        @pl.when(j == 1)
        def _():
            for load in loads:
                load.wait()

        @pl.when(j >= 1)
        def _():
            use_piece(j - 1)

        return carry

    lax.fori_loop(0, PIECES + 1, step, 0)

    def finish(t, carry):
        rows = pl.ds(pl.multiple_of(t * MSG, 16), MSG)
        g = acc[0, rows, :]
        act[rows, :] = (g / (1.0 + jnp.exp(-g)) * acc[1, rows, :]).astype(BF16)
        return carry

    lax.fori_loop(0, ROWS // MSG, finish, 0)

    for j in (PIECES - 2, PIECES - 1):
        for k, o in enumerate(OFFSETS):
            message(k, j, to_plane(o), here).wait_send()

    def sent_columns(j, carry):
        for n, o in enumerate(COLUMN):
            column_copy(n, j, to_column(o), me).wait_send()
        return carry

    lax.fori_loop(0, PIECES, sent_columns, 0)


def dispatch(normed, code, weight, w_gate, w_up):
    vmem = pl.BlockSpec(memory_space=pltpu.VMEM)
    hbm = pl.BlockSpec(memory_space=pl.ANY)
    dma = pltpu.SemaphoreType.DMA
    return pl.pallas_call(
        dispatch_kernel,
        name="dispatch",
        out_shape=[
            jax.ShapeDtypeStruct((ROWS, FF), BF16),
            jax.ShapeDtypeStruct((8, PLANE, TOK), F32),
            jax.ShapeDtypeStruct((8, PLANE, TOK), F32),
        ],
        in_specs=[vmem, vmem, vmem, hbm, hbm],
        out_specs=[vmem] * 3,
        scratch_shapes=[
            pltpu.VMEM((PIECES, 8 * TOK, PIECE), BF16),
            pltpu.VMEM((8, PLANE, TOK), BF16),
            pltpu.VMEM((8, PLANE, TOK), BF16),
            pltpu.VMEM((ALL, 8 * TOK), BF16),
            pltpu.VMEM((2, ALL, PIECE), BF16),
            pltpu.VMEM((PIECES, 2, ROWS, PIECE), BF16),
            pltpu.VMEM((D, FF), BF16),
            pltpu.VMEM((D, FF), BF16),
            pltpu.VMEM((2, ROWS, FF), F32),
            dma((2,)),
            dma((2, len(COLUMN))),
            dma((2, len(COLUMN))),
            dma((PIECES, len(COLUMN))),
            dma((PIECES, len(COLUMN))),
            dma((PIECES, len(OFFSETS))),
            dma((PIECES, len(OFFSETS))),
        ],
        compiler_params=pltpu.CompilerParams(
            collective_id=2, has_side_effects=True, vmem_limit_bytes=60 * 2**20
        ),
    )(normed, code.reshape(4, PLANE, TOK), weight.reshape(4, PLANE, TOK), w_gate, w_up)


def combine_kernel(
    act, codes, weights, w_down, hidden, out,
    wd, answers, got, mix, partial, sums,
    wsem, msg_s, msg_r, col_s, col_r,
):
    x, y, z, c = coords()
    load = pltpu.make_async_copy(w_down, wd, wsem.at[0])
    load.start()
    greet_all()
    load.wait()
    here = (x, y, z, c)
    me = z * 2 + c

    def message(k, j, dev, src_dev):
        chip = dev[0] * 4 + dev[1]
        of = plane_index(src_dev[0], src_dev[1], src_dev[3])
        return pltpu.make_async_remote_copy(
            src_ref=answers.at[j, dev[3], pl.ds(pl.multiple_of(chip * MSG, 16), MSG)],
            dst_ref=got.at[j, pl.ds(pl.multiple_of(of * MSG, 16), MSG)],
            send_sem=msg_s.at[j, k], recv_sem=msg_r.at[j, k],
            device_id=device(*dev), device_id_type=MESH,
        )

    def column_copy(n, j, dev, src_dev):
        block = dev[2] * 2 + dev[3]
        return pltpu.make_async_remote_copy(
            src_ref=partial.at[j, pl.ds(pl.multiple_of(block * TOK, TOK), TOK)],
            dst_ref=sums.at[j, src_dev[2], src_dev[3]],
            send_sem=col_s.at[j, n], recv_sem=col_r.at[j, n],
            device_id=device(*dev), device_id_type=MESH,
        )

    own_rows = pl.ds(pl.multiple_of(plane_index(x, y, c) * MSG, 16), MSG)
    own_place = pl.ds(pl.multiple_of((x * 4 + y) * MSG, 16), MSG)

    def send_piece(j, carry):
        for half in range(2):
            span = pl.ds(pl.multiple_of(half * HALF + j * PIECE, PIECE), PIECE)

            def tile(t, inner):
                rows = pl.ds(pl.multiple_of(t * (ROWS // 4), 16), ROWS // 4)
                answers[j, half, rows, :] = jnp.dot(act[rows, :], wd[:, span], preferred_element_type=F32).astype(BF16)
                return inner

            lax.fori_loop(0, 4, tile, 0)
        for k, o in enumerate(OFFSETS):
            message(k, j, to_plane(o), here).start()
        got[j, own_rows, :] = answers[j, c, own_place, :]
        return carry

    lax.fori_loop(0, PIECES, send_piece, 0)

    block, place = table_rows()

    def fill(p, carry):
        for b in range(8):
            rows = []
            for n in range(8):
                l = p * 8 + n
                hit = (codes[b, pl.ds(l, 1), :] == place) & (block == b)
                rows.append(jnp.where(hit, weights[b, pl.ds(l, 1), :], 0.0))
            whole = jnp.concatenate(rows, axis=0)
            mix[b * TOK : (b + 1) * TOK, pl.ds(pl.multiple_of(p * 8 * MSG, TOK), 8 * MSG)] = whole.T.astype(BF16)
        return carry

    lax.fori_loop(0, PLANE // 8, fill, 0)

    def reduce_piece(j):
        for k, o in enumerate(OFFSETS):
            message(k, j, here, from_plane(o)).wait_recv()

        def tile(t, carry):
            rows = pl.ds(pl.multiple_of(t * 256, 256), 256)
            partial[j, rows, :] = jnp.dot(mix[rows, :], got[j], preferred_element_type=F32).astype(BF16)
            return carry

        lax.fori_loop(0, 4, tile, 0)
        for n, o in enumerate(COLUMN):
            column_copy(n, j, to_column(o), here).start()
        sums[j, z, c] = partial[j, pl.ds(pl.multiple_of(me * TOK, TOK), TOK), :]

    def finish_piece(j):
        for n, o in enumerate(COLUMN):
            column_copy(n, j, here, from_column(o)).wait_recv()
        for half in range(2):
            span = pl.ds(pl.multiple_of(half * HALF + j * PIECE, PIECE), PIECE)
            total = hidden[:, span]
            for n in range(4):
                total = total + sums[j, n, half].astype(F32)
            out[:, span] = total.astype(BF16)

    def step(j, carry):
        @pl.when(j < PIECES)
        def _():
            reduce_piece(j)

        @pl.when(j >= 1)
        def _():
            finish_piece(j - 1)

        return carry

    lax.fori_loop(0, PIECES + 1, step, 0)

    def sent(j, carry):
        for k, o in enumerate(OFFSETS):
            message(k, j, to_plane(o), here).wait_send()
        for n, o in enumerate(COLUMN):
            column_copy(n, j, to_column(o), here).wait_send()
        return carry

    lax.fori_loop(0, PIECES, sent, 0)


def combine(act, codes, weights, w_down, hidden):
    vmem = pl.BlockSpec(memory_space=pltpu.VMEM)
    dma = pltpu.SemaphoreType.DMA
    return pl.pallas_call(
        combine_kernel,
        name="combine",
        out_shape=jax.ShapeDtypeStruct((TOK, D), BF16),
        in_specs=[vmem, vmem, vmem, pl.BlockSpec(memory_space=pl.ANY), vmem],
        out_specs=vmem,
        scratch_shapes=[
            pltpu.VMEM((FF, D), BF16),
            pltpu.VMEM((PIECES, 2, ROWS, PIECE), BF16),
            pltpu.VMEM((PIECES, ALL, PIECE), BF16),
            pltpu.VMEM((8 * TOK, ALL), BF16),
            pltpu.VMEM((PIECES, 8 * TOK, PIECE), BF16),
            pltpu.VMEM((PIECES, 4, 2, TOK, PIECE), BF16),
            dma((1,)),
            dma((PIECES, len(OFFSETS))),
            dma((PIECES, len(OFFSETS))),
            dma((PIECES, len(COLUMN))),
            dma((PIECES, len(COLUMN))),
        ],
        compiler_params=pltpu.CompilerParams(
            collective_id=3, has_side_effects=True, vmem_limit_bytes=60 * 2**20
        ),
    )(act, codes, weights, w_down, hidden)


def body(
    queries, fresh_keys, fresh_values, stored_keys, stored_values, column_blocks, diagonal_offsets,
    residual, norm_gain, routes, gate_weights, w_gate, w_up, w_down,
):
    kv = exchange(*collect(column_blocks, diagonal_offsets, stored_keys, stored_values))
    hidden, normed, code, weight = attend(
        column_blocks, diagonal_offsets, queries, fresh_keys, fresh_values, kv,
        residual, norm_gain, routes, gate_weights,
    )
    act, codes, weights = dispatch(normed, code, weight, w_gate[0], w_up[0])
    return combine(act, codes, weights, w_down[0], hidden)


def solution(mesh):
    rows = P(("ctx", "exp"), None)
    experts = P(("ctx", "exp"), None, None)
    in_specs = (
        rows, rows, rows, P("ctx", None), P("ctx", None), P(), P(), rows, P(), rows, rows,
        experts, experts, experts,
    )
    return jax.shard_map(body, mesh=mesh, in_specs=in_specs, out_specs=rows, check_vma=False)
```

time: 803 us -> 346 us (0.43)
  the two profiles are of different devices: /device:TPU:86 before, /device:TPU:5 now
where the time goes in v1:
time: 346 us
  Pallas kernels  335 us (97%)
  local copies, waits for them, and re-layouts  11.2 us (3%)
    pallas_call x1, Pallas kernels, combine(): pl.pallas_call(combine_kernel, name='combine', out_shape=jax.ShapeDtypeSt...  157 us
    pallas_call x1, Pallas kernels, dispatch(): pl.pallas_call(dispatch_kernel, name='dispatch', out_shape=[jax.ShapeDtyp...  154 us
    pallas_call x1, Pallas kernels, exchange(): pl.pallas_call(exchange_kernel, name='key_exchange', out_shape=jax.ShapeD...  16.5 us
    unnamed x33, local copies, waits for them, and re-layouts  11.2 us

profile of v1, /device:TPU:5, one launch (start us, length us, event | category | flops | bytes accessed | tf_op | source)
XLA Modules:
  0.0 345.9 jit_solution(9722466268866570804)
XLA Ops:
  0.0 0.8 copy.15.routes
  0.8 0.8 copy.16.gates
  1.6 0.0 copy-start.3
  1.6 1.2 copy-done.3
  2.8 0.0 copy-start.4
  2.8 1.2 copy-done.4
  4.0 0.0 copy-start.11
  4.0 0.7 copy-done.11
  4.7 0.0 copy-start.13
  4.7 0.7 copy-done.13
  5.4 0.0 copy-start.1
  5.4 0.0 copy-start.10
  5.4 0.0 copy-start.12
  5.4 0.0 copy-start.14
  5.4 0.9 collect_blocks.1
  6.4 16.5 %key_exchange.1.kv = bf16[2,2,1152,128]{3,2,1,0:T(8,128)(2,1)S(1)} custom-call(bf16[2,2,1152,128]{3,2,1,0:T(8,128)(2,1)S(1)} %get-tuple-element.14.con, f32[36,8,128]{2,1,0:T(8,128)S(1)} %get-tuple-element.15.near), custom_call_target="tpu_custom_call" | custom-call | tf_op jit(solution)/shard_map/key_exchange/pallas_call | solution.py:256
  22.9 0.0 copy-done.1
  22.9 0.0 copy-done.2
  22.9 0.0 copy-done.6
  22.9 0.0 copy-done.7
  22.9 0.0 copy-done.10
  22.9 0.0 copy-done.12
  22.9 0.0 copy-done.14
  23.0 6.4 %attention.1 = (f32[128,4096]{1,0:T(8,128)S(1)}, bf16[128,4096]{1,0:T(8,128)(2,1)S(1)}, bf16[128,128]{1,0:T(8,128)(2,1)S(1)}, bf16[128,128]{1,0:T(8,128)(2,1)S(1)}) custom-call(s32[2,2]{1,0:T(2,128)S(1)} %copy-done.12, s32[2,8]{1,0:T(2,128)S(1)} %copy-done.14, bf16[128,4096]{1,0:T(8,128)(2,1)S(1)} %copy-done.1, bf16[128,256]{1,0:T(8,128)(2,1)S(1)} %copy-done.6, ...), custom_call_target="tpu_custom_call" | custom-call | tf_op jit(solution)/shard_map/attention/pallas_call | solution.py:340
  29.3 0.0 copy-start
  29.3 1.3 copy-done
  30.7 1.0 copy-done.5
  31.6 0.6 copy-done.8
  32.2 0.6 copy-done.9
  32.8 153.9 %dispatch.1 = (bf16[1280,768]{1,0:T(8,128)(2,1)}, f32[8,32,128]{2,1,0:T(8,128)}, f32[8,32,128]{2,1,0:T(8,128)}) custom-call(bf16[128,4096]{1,0:T(8,128)(2,1)} %copy-done.5, bf16[4,32,128]{2,1,0:T(8,128)(2,1)} %bitcast.6, bf16[4,32,128]{2,1,0:T(8,128)(2,1)} %bitcast.7, bf16[4096,768]{1,0:T(8,128)(2,1)} %bitcast.10, bf16[4096,768]{1,0:T(8,128)(2,1)} %bitcast.11), custom_call_target="tpu_custom_call" | custom-call | tf_op jit(solution)/shard_map/dispatch/pallas_call | solution.py:530
  186.7 156.9 %combine.1 = bf16[128,4096]{1,0:T(8,128)(2,1)} custom-call(bf16[1280,768]{1,0:T(8,128)(2,1)} %get-tuple-element.19.act, f32[8,32,128]{2,1,0:T(8,128)} %get-tuple-element.20.codes, f32[8,32,128]{2,1,0:T(8,128)} %get-tuple-element.21.weights, bf16[768,4096]{1,0:T(8,128)(2,1)} %bitcast.9, f32[128,4096]{1,0:T(8,128)} %copy-done), custom_call_target="tpu_custom_call" | custom-call | tf_op jit(solution)/shard_map/combine/pallas_call | solution.py:681
  343.6 2.3 copy.18
  (6 shorter events, 0.0 us)
Async XLA Ops:
  1.6 1.2 copy-start.3
  2.8 1.2 copy-start.4
  4.0 0.7 copy-start.11
  4.7 0.7 copy-start.13
  5.4 17.5 %copy-start.1 = (bf16[128,4096]{1,0:T(8,128)(2,1)S(1)}, bf16[128,4096]{1,0:T(8,128)(2,1)}, u32[]{:S(2)}) copy-start(bf16[128,4096]{1,0:T(8,128)(2,1)} %q.1) | copy-start | bytes 3145732
  5.4 17.5 %copy-start.2 = (bf16[128,4096]{1,0:T(8,128)(2,1)S(1)}, bf16[128,4096]{1,0:T(8,128)(2,1)}, u32[]{:S(2)}) copy-start(bf16[128,4096]{1,0:T(8,128)(2,1)} %res.1) | copy-start | bytes 3145732
  5.4 17.5 %copy-start.6 = (bf16[128,256]{1,0:T(8,128)(2,1)S(1)}, bf16[128,256]{1,0:T(8,128)(2,1)}, u32[]{:S(2)}) copy-start(bf16[128,256]{1,0:T(8,128)(2,1)} %fk.1) | copy-start | bytes 196612
  5.4 17.5 %copy-start.7 = (bf16[128,256]{1,0:T(8,128)(2,1)S(1)}, bf16[128,256]{1,0:T(8,128)(2,1)}, u32[]{:S(2)}) copy-start(bf16[128,256]{1,0:T(8,128)(2,1)} %fv.1) | copy-start | bytes 196612
  5.4 17.5 %copy-start.10 = (f32[4096]{0:T(1024)S(1)}, f32[4096]{0:T(1024)}, u32[]{:S(2)}) copy-start(f32[4096]{0:T(1024)} %param.22) | copy-start | bytes 49156
  5.4 17.5 %copy-start.12 = (s32[2,2]{1,0:T(2,128)S(1)}, s32[2,2]{1,0:T(2,128)}, u32[]{:S(2)}) copy-start(s32[2,2]{1,0:T(2,128)} %cols.3) | copy-start | bytes 52
  5.4 17.5 %copy-start.14 = (s32[2,8]{1,0:T(2,128)S(1)}, s32[2,8]{1,0:T(2,128)}, u32[]{:S(2)}) copy-start(s32[2,8]{1,0:T(2,128)} %offs.3) | copy-start | bytes 196
  29.3 1.3 copy-start
  30.7 1.0 copy-start.5
  31.6 0.6 copy-start.8
  32.2 0.6 copy-start.9

commit v2 on v1

v2 whole, which is shorter than its diff:
```python
import functools

import jax
import jax.numpy as jnp
from jax import lax
from jax.experimental import pallas as pl
from jax.experimental.pallas import tpu as pltpu
from jax.sharding import PartitionSpec as P

MESH = pl.DeviceIdType.MESH
BF16 = jnp.bfloat16
F32 = jnp.float32
BLOCK = 64
HEAD = 128
HEADS_KV = 2
GROUP = 16
VERT = 2
SLASH = 8
SLOTS = VERT + 2 * SLASH
TOK = 128
D = 4096
FF = 768
HALF = D // 2
CAP = 10
PLANE = 32
MSG = 8 * CAP
ROWS = 16 * MSG
ALL = PLANE * MSG
PIECE = 256
PIECES = HALF // PIECE
NEG = -1e30


TYPES = 3


def coords():
    ctx = lax.axis_index("ctx")
    exp = lax.axis_index("exp")
    return ((exp // 4) % 2) * 2 + ctx // 2, exp % 4, exp // 8, ctx % 2


def device(x, y, z, c):
    return ((x % 2) * 2 + c, z * 8 + (x // 2) * 4 + y)


def unit(t):
    return (2 - t) * (1 - t) // 2, t * (2 - t), t * (t - 1) // 2


def turned(t):
    x, y, z, c = coords()
    t0, t1, t2 = unit(t)
    return x * (t0 + t1) + y * t2, y * t0 + z * (t1 + t2), z * t0 + y * t1 + x * t2, c


def turned_device(t, dev):
    p, q, a, c = dev
    t0, t1, t2 = unit(t)
    return device(p * (t0 + t1) + a * t2, q * t0 + a * t1 + p * t2, a * t0 + q * (t1 + t2), c)


def plane_index(dev):
    return (dev[0] * 4 + dev[1]) * 2 + dev[3]


def ordered_offsets():
    left = [(dx, dy, dc) for dx in range(4) for dy in range(4) for dc in range(2) if dx or dy or dc]
    use = {}
    out = []

    def links(o):
        found = []
        for axis in range(2):
            if o[axis] == 1:
                found.append((axis, 1))
            elif o[axis] == 3:
                found.append((axis, -1))
            elif o[axis] == 2:
                found += [(axis, 1), (axis, -1)]
        return found

    while left:
        best = min(left, key=lambda o: (sum(2 * use.get(k, 0) + 1 for k in links(o)), -len(links(o)), o))
        left.remove(best)
        out.append(best)
        for k in links(best):
            use[k] = use.get(k, 0) + 1
    return out


OFFSETS = ordered_offsets()
COLUMN = [(1, 0), (3, 1), (2, 0), (3, 0), (1, 1), (2, 1), (0, 1)]
PEERS = [
    (dx, dy, dz, dc)
    for dx in range(4)
    for dy in range(4)
    for dz in range(4)
    for dc in range(2)
    if dx * dy * dz == 0 and (dx or dy or dz or dc)
]


def to_plane(o, dev):
    return (dev[0] + o[0]) % 4, (dev[1] + o[1]) % 4, dev[2], (dev[3] + o[2]) % 2


def from_plane(o, dev):
    return (dev[0] + 4 - o[0]) % 4, (dev[1] + 4 - o[1]) % 4, dev[2], (dev[3] + 2 - o[2]) % 2


def to_column(o, dev):
    return dev[0], dev[1], (dev[2] + o[0]) % 4, (dev[3] + o[1]) % 2


def from_column(o, dev):
    return dev[0], dev[1], (dev[2] + 4 - o[0]) % 4, (dev[3] + 2 - o[1]) % 2


def greet_all():
    bar = pltpu.get_barrier_semaphore()
    x, y, z, c = coords()
    for o in PEERS:
        other = device((x + o[0]) % 4, (y + o[1]) % 4, (z + o[2]) % 4, (c + o[3]) % 2)
        pl.semaphore_signal(bar, inc=1, device_id=other, device_id_type=MESH)
    pl.semaphore_wait(bar, len(PEERS))


def digits(row):
    n = (row * 3277) >> 16
    return n >> 4, (n >> 2) & 3, n & 3, row - n * 20


def swap_matrix():
    row = lax.broadcasted_iota(jnp.int32, (320, 1), 0)
    _, d2, d1, rest = digits(row)
    source = d1 * 80 + d2 * 20 + rest
    return (lax.broadcasted_iota(jnp.int32, (320, 320), 1) == source).astype(F32).astype(BF16)


def turn_matrix(rows, start, back):
    row = lax.broadcasted_iota(jnp.int32, (rows, 1), 0) + start
    d3, d2, d1, rest = digits(row)
    source = d1 * 320 + d3 * 80 + d2 * 20 + rest if back else d2 * 320 + d1 * 80 + d3 * 20 + rest
    return (lax.broadcasted_iota(jnp.int32, (rows, ROWS), 1) == source).astype(F32).astype(BF16)


def side(h):
    exp = lax.axis_index("exp")
    return exp + h * (4 - 8 * ((exp // 4) % 2))


def collect_kernel(cols, offs, keys_hbm, values_hbm, con, near, keys, values, sem):
    loads = [pltpu.make_async_copy(keys_hbm, keys, sem.at[0]), pltpu.make_async_copy(values_hbm, values, sem.at[1])]
    for load in loads:
        load.start()
    ctx = lax.axis_index("ctx")
    xl = ctx // 2
    for load in loads:
        load.wait()

    def put(h, slot, block_a, block_b):
        near_a = block_a - 32 * ctx
        near_b = block_b - 32 * ctx
        local = jnp.where((near_a >= 0) & (near_a < 32), near_a, near_b)
        inside = (local >= 0) & (local < 32)
        start = pl.multiple_of(jnp.clip(local, 0, 31) * BLOCK, BLOCK)
        factor = jnp.where(inside, 1.0, 0.0).astype(BF16)
        for kind, ref in ((0, keys), (1, values)):
            block = ref[pl.ds(start, BLOCK), h * HEAD : (h + 1) * HEAD]
            con[kind, h, slot * BLOCK : (slot + 1) * BLOCK, :] = block * factor

    for h in range(HEADS_KV):
        exp = jnp.where(xl == 0, side(h), side(0))
        for v in range(VERT):
            put(h, v, cols[h, v], cols[h, v])
            here = (cols[h, v] // 64) == xl
            near[h * SLOTS + v] = jnp.full((8, HEAD), jnp.where(here, 1.0, 0.0), F32)
        for i in range(2):
            for s in range(SLASH):
                block_2 = 256 + 2 * exp + i - offs[h, s]
                slot = VERT + i * SLASH + s
                put(h, slot, block_2, block_2 + 64)
                near[h * SLOTS + slot] = jnp.full((8, HEAD), jnp.where(block_2 >= 0, 1.0, 0.0), F32)


def collect(cols, offs, keys, values):
    return pl.pallas_call(
        collect_kernel,
        name="collect_blocks",
        out_shape=[
            jax.ShapeDtypeStruct((2, HEADS_KV, SLOTS * BLOCK, HEAD), BF16),
            jax.ShapeDtypeStruct((HEADS_KV * SLOTS, 8, HEAD), F32),
        ],
        in_specs=[pl.BlockSpec(memory_space=pltpu.SMEM)] * 2 + [pl.BlockSpec(memory_space=pltpu.HBM)] * 2,
        out_specs=[pl.BlockSpec(memory_space=pltpu.VMEM)] * 2,
        scratch_shapes=[
            pltpu.VMEM((2048, HEADS_KV * HEAD), BF16),
            pltpu.VMEM((2048, HEADS_KV * HEAD), BF16),
            pltpu.SemaphoreType.DMA((2,)),
        ],
        compiler_params=pltpu.CompilerParams(vmem_limit_bytes=16 * 2**20),
    )(cols, offs, keys, values)


def exchange_kernel(con, near, out, sib, chip, rem, fin, arr, ssem, rsem):
    x, y, z, c = coords()
    xl = x % 2
    exp = lax.axis_index("exp")
    twin = (xl * 2 + 1 - c, exp)
    across = [((1 - xl) * 2 + c, side(h)) for h in range(HEADS_KV)]
    bar = pltpu.get_barrier_semaphore()
    for other in (twin, *across):
        pl.semaphore_signal(bar, inc=1, device_id=other, device_id_type=MESH)
    pl.semaphore_wait(bar, 3)

    first = pltpu.make_async_remote_copy(
        src_ref=con.at[1 - c], dst_ref=sib, send_sem=ssem.at[0], recv_sem=rsem.at[0],
        device_id=twin, device_id_type=MESH,
    )
    first.start()
    first.wait()
    chip[...] = con[c] + sib[...]

    verts = VERT * BLOCK

    def whole(h):
        return pltpu.make_async_remote_copy(
            src_ref=chip.at[h], dst_ref=rem.at[h], send_sem=ssem.at[1 + h], recv_sem=rsem.at[1 + h],
            device_id=across[h], device_id_type=MESH,
        )

    def vertical(h):
        return pltpu.make_async_remote_copy(
            src_ref=chip.at[h, pl.ds(0, verts)], dst_ref=rem.at[h, pl.ds(0, verts)],
            send_sem=ssem.at[1 + h], recv_sem=rsem.at[1 + h],
            device_id=across[h], device_id_type=MESH,
        )

    @pl.when(xl == 0)
    def _():
        for h in range(HEADS_KV):
            whole(h).start()

    @pl.when(xl == 1)
    def _():
        for h in range(HEADS_KV):
            vertical(h).start()

    def back(h):
        return pltpu.make_async_remote_copy(
            src_ref=fin.at[h], dst_ref=arr.at[h], send_sem=ssem.at[3 + h], recv_sem=rsem.at[3 + h],
            device_id=twin, device_id_type=MESH,
        )

    def pick(h, slot):
        span = slice(slot * BLOCK, (slot + 1) * BLOCK)
        local = near[h * SLOTS + slot, 0:1, :].astype(BF16)
        far = rem[h, span, :]
        return span, chip[h, span, :] * local + far * (1.0 - local).astype(BF16), far

    def pick_verticals(h):
        for v in range(VERT):
            span, mixed, _ = pick(h, v)
            fin[h, span, :] = mixed
            out[c, h, span, :] = mixed

    for h in range(HEADS_KV):

        @pl.when(xl == 0)
        def _():
            vertical(h).wait_recv()
            pick_verticals(h)
            fin[h, verts:, :] = jnp.zeros((2 * SLASH * BLOCK, HEAD), BF16)
            out[c, h, verts:, :] = jnp.zeros((2 * SLASH * BLOCK, HEAD), BF16)

        @pl.when(xl == 1)
        def _():
            whole(h).wait_recv()
            pick_verticals(h)
            for slot in range(VERT, SLOTS):
                span, mixed, far = pick(h, slot)

                @pl.when(c == 1)
                def _():
                    out[1, h, span, :] = mixed
                    fin[h, span, :] = far

                @pl.when(c == 0)
                def _():
                    out[0, h, span, :] = far
                    fin[h, span, :] = mixed

        back(h).start()

    for h in range(HEADS_KV):
        back(h).wait()
        out[1 - c, h] = arr[h]

    @pl.when(xl == 0)
    def _():
        for h in range(HEADS_KV):
            whole(h).wait_send()

    @pl.when(xl == 1)
    def _():
        for h in range(HEADS_KV):
            vertical(h).wait_send()


def exchange(con, near):
    part = (HEADS_KV, SLOTS * BLOCK, HEAD)
    return pl.pallas_call(
        exchange_kernel,
        name="key_exchange",
        out_shape=jax.ShapeDtypeStruct((2,) + part, BF16),
        in_specs=[pl.BlockSpec(memory_space=pltpu.VMEM)] * 2,
        out_specs=pl.BlockSpec(memory_space=pltpu.VMEM),
        scratch_shapes=[
            pltpu.VMEM(part, BF16),
            pltpu.VMEM(part, BF16),
            pltpu.VMEM(part, BF16),
            pltpu.VMEM(part, BF16),
            pltpu.VMEM(part, BF16),
            pltpu.SemaphoreType.DMA((5,)),
            pltpu.SemaphoreType.DMA((5,)),
        ],
        compiler_params=pltpu.CompilerParams(
            collective_id=1, has_side_effects=True, vmem_limit_bytes=24 * 2**20
        ),
    )(con, near)


def attend_kernel(
    cols, offs, q, fk, fv, kv, res, gain, routes, gates, hidden_out, normed_out, table_out,
    hidden, normed, table, sem,
):
    puts = []

    def put(src, dst):
        copy = pltpu.make_async_copy(src, dst, sem.at[len(puts)])
        copy.start()
        puts.append(copy)

    ctx = lax.axis_index("ctx")
    exp = lax.axis_index("exp")

    ids = routes[...]
    group, rest = ids >> 5, ids & 31
    ex, ey, ez, ec = ((rest >> 2) & 1) * 2 + (group >> 1), rest & 3, rest >> 3, group & 1
    lanes = lax.broadcasted_iota(jnp.int32, (TOK, TOK), 1)
    subs = lax.broadcasted_iota(jnp.int32, (TOK, TOK), 0)
    later = (subs < lanes).astype(F32).astype(BF16)
    for t, (p, r, a) in enumerate(((ex, ey, ez), (ex, ez, ey), (ey, ez, ex))):
        number = a * PLANE + (p * 4 + r) * 2 + ec
        named = jnp.zeros((TOK, TOK), F32)
        strength = jnp.zeros((TOK, TOK), F32)
        for n in range(8):
            hit = number[n : n + 1, :] == subs
            named = named + jnp.where(hit, 1.0, 0.0)
            strength = strength + jnp.where(hit, gates[n : n + 1, :], 0.0)
        place = jnp.dot(named.astype(BF16), later, preferred_element_type=F32)
        place = jnp.where(named > 0.5, place, -1.0).astype(BF16)
        strength = strength.astype(BF16)
        for n in range(4):
            table[t, n, 0] = place[n * PLANE : (n + 1) * PLANE]
            table[t, n, 1] = strength[n * PLANE : (n + 1) * PLANE]
    put(table, table_out)

    scale = 1.0 / HEAD**0.5
    lane = lax.broadcasted_iota(jnp.int32, (1, (VERT + SLASH) * BLOCK), 1) // BLOCK
    heads = 4
    ones = jnp.ones(((VERT + SLASH) * BLOCK, HEAD), BF16)
    for h in range(HEADS_KV):
        for i in range(2):
            block = 128 + 2 * (ctx * 32 + exp) + i
            listed = [cols[h, v] for v in range(VERT)] + [block - offs[h, s] for s in range(SLASH)]
            bias = jnp.zeros(lane.shape, F32)
            for n, one in enumerate(listed):
                kept = (one >= 0) & (one < 128)
                for before in listed[:n]:
                    kept = kept & (one != before)
                bias = jnp.where(lane == n, jnp.where(kept, 0.0, NEG), bias)
            slash = VERT * BLOCK + i * SLASH * BLOCK
            k = jnp.concatenate([kv[0, h, : VERT * BLOCK, :], kv[0, h, slash : slash + SLASH * BLOCK, :]], axis=0)
            v = jnp.concatenate([kv[1, h, : VERT * BLOCK, :], kv[1, h, slash : slash + SLASH * BLOCK, :]], axis=0)
            v = jnp.concatenate([v, ones], axis=1)
            rows = slice(i * BLOCK, (i + 1) * BLOCK)
            own_k = fk[rows, h * HEAD : (h + 1) * HEAD].astype(F32)
            own_v = fv[rows, h * HEAD : (h + 1) * HEAD].astype(F32)
            own_k = jnp.concatenate([own_k] * heads, axis=0)
            own_v = jnp.concatenate([own_v] * heads, axis=0)
            for g in range(0, GROUP, heads):
                spans = [slice((h * GROUP + g + n) * HEAD, (h * GROUP + g + n + 1) * HEAD) for n in range(heads)]
                part = jnp.concatenate([q[rows, span] for span in spans], axis=0)
                scores = lax.dot_general(part, k, (((1,), (1,)), ((), ())), preferred_element_type=F32)
                scores = scores * scale + bias
                own = jnp.sum(part.astype(F32) * own_k, axis=1, keepdims=True) * scale
                top = jnp.maximum(own, jnp.max(scores, axis=1, keepdims=True))
                weights = jnp.exp(scores - top).astype(BF16)
                own_weight = jnp.exp(own - top).astype(BF16).astype(F32)
                both = jnp.dot(weights, v, preferred_element_type=F32)
                numer = both[:, :HEAD] + own_weight * own_v
                denom = both[:, HEAD:] + own_weight
                attended = numer / denom
                for n, span in enumerate(spans):
                    hidden[rows, span] = res[rows, span].astype(F32) + attended[n * BLOCK : (n + 1) * BLOCK]
            done = hidden.at[pl.ds(i * BLOCK, BLOCK), pl.ds(h * GROUP * HEAD, GROUP * HEAD)]
            put(done, hidden_out.at[pl.ds(i * BLOCK, BLOCK), pl.ds(h * GROUP * HEAD, GROUP * HEAD)])

    for r in range(0, TOK, 16):
        part = hidden[r : r + 16, :]
        spread = jnp.mean(part * part, axis=1, keepdims=True)
        normed[r : r + 16, :] = (part * lax.rsqrt(spread + 1e-6) * gain[...]).astype(BF16)

    put(normed, normed_out)
    for copy in puts:
        copy.wait()


def attend(cols, offs, q, fk, fv, kv, res, gain, routes, gates):
    vmem = pl.BlockSpec(memory_space=pltpu.VMEM)
    shapes = [((TOK, D), F32), ((TOK, D), BF16), ((TYPES, 4, 2, PLANE, TOK), BF16)]
    return pl.pallas_call(
        attend_kernel,
        name="attention",
        out_shape=[jax.ShapeDtypeStruct(*one) for one in shapes],
        in_specs=[pl.BlockSpec(memory_space=pltpu.SMEM)] * 2 + [vmem] * 8,
        out_specs=[pl.BlockSpec(memory_space=pltpu.HBM)] * 3,
        scratch_shapes=[pltpu.VMEM(*one) for one in shapes] + [pltpu.SemaphoreType.DMA((6,))],
        compiler_params=pltpu.CompilerParams(vmem_limit_bytes=32 * 2**20),
    )(cols, offs, q, fk, fv, kv, res, gain.reshape(1, D), routes.T, gates.T)


def table_rows():
    row = lax.broadcasted_iota(jnp.int32, (MSG, TOK), 0)
    block = jnp.zeros((MSG, TOK), jnp.int32)
    for b in range(1, 8):
        block = block + jnp.where(row >= b * CAP, 1, 0)
    return block, (row - block * CAP).astype(F32)


def dispatch_kernel(
    normed_hbm, table_hbm, w_gate, w_up, act, tables_out,
    normed, table, x_all, tables, select, stage, got, weights, acc, swap, turn, sorted_rows,
    in_sem, w_sem, tab_s, tab_r, col_s, col_r, msg_s, msg_r,
):
    loads = [
        pltpu.make_async_copy(table_hbm, table, in_sem.at[0]),
        pltpu.make_async_copy(normed_hbm, normed, in_sem.at[1]),
    ]
    for load in loads:
        load.start()

    def weight_loads(j):
        return [
            pltpu.make_async_copy(
                w.at[pl.ds(pl.multiple_of(half * HALF + j * PIECE, PIECE), PIECE)],
                weights.at[j % 2, n, half],
                w_sem.at[j % 2, n, half],
            )
            for n, w in enumerate((w_gate, w_up))
            for half in range(2)
        ]

    for j in range(2):
        for load in weight_loads(j):
            load.start()
    greet_all()
    for load in loads:
        load.wait()

    def table_copy(n, t, dev, slot):
        return pltpu.make_async_remote_copy(
            src_ref=table.at[t, dev[2]], dst_ref=tables.at[t, slot], send_sem=tab_s.at[t, n], recv_sem=tab_r.at[t, n],
            device_id=turned_device(t, dev), device_id_type=MESH,
        )

    def column_copy(n, j, t, dev, slot):
        start = pl.multiple_of(dev[3] * HALF + j * PIECE, PIECE)
        return pltpu.make_async_remote_copy(
            src_ref=normed.at[:, pl.ds(start, PIECE)],
            dst_ref=x_all.at[j, pl.ds(pl.multiple_of(slot * TOK, TOK), TOK)],
            send_sem=col_s.at[j, n], recv_sem=col_r.at[j, n],
            device_id=turned_device(t, dev), device_id_type=MESH,
        )

    for t in range(TYPES):
        here = turned(t)
        me = here[2] * 2 + here[3]
        for n, o in enumerate(COLUMN):
            table_copy(n, t, to_column(o, here), me).start()
        tables[t, me] = table[t, here[2]]

    def send_columns(j, carry):
        t = j % 3
        here = turned(t)
        me = here[2] * 2 + here[3]
        for n, o in enumerate(COLUMN):
            column_copy(n, j, t, to_column(o, here), me).start()
        start = pl.multiple_of(here[3] * HALF + j * PIECE, PIECE)
        x_all[j, pl.ds(pl.multiple_of(me * TOK, TOK), TOK), :] = normed[:, pl.ds(start, PIECE)]
        return carry

    lax.fori_loop(0, PIECES, send_columns, 0)

    for t in range(TYPES):
        here = turned(t)
        for n, o in enumerate(COLUMN):
            dev = from_column(o, here)
            table_copy(n, t, dev, dev[2] * 2 + dev[3]).wait()
    tables_out[...] = tables[...].astype(F32)

    block, place = table_rows()

    def fill(t):
        def one(l, carry):
            for b in range(8):
                row = tables_out[t, b, 0, pl.ds(l, 1), :]
                hit = (row == place) & (block == b)
                select[t, pl.ds(pl.multiple_of(l * MSG, 16), MSG), b * TOK : (b + 1) * TOK] = jnp.where(
                    hit, 1.0, 0.0
                ).astype(BF16)
            return carry

        lax.fori_loop(0, PLANE, one, 0)

    fill(0)

    def message(k, j, t, dev, src_dev):
        chip = src_dev[0] * 4 + src_dev[1]
        return pltpu.make_async_remote_copy(
            src_ref=stage.at[j % 2, pl.ds(pl.multiple_of(plane_index(dev) * MSG, 16), MSG)],
            dst_ref=got.at[j, src_dev[3], pl.ds(pl.multiple_of(chip * MSG, 16), MSG)],
            send_sem=msg_s.at[j, k], recv_sem=msg_r.at[j, k],
            device_id=turned_device(t, dev), device_id_type=MESH,
        )

    def sent(j):
        here = turned(j % 3)
        for k, o in enumerate(OFFSETS):
            message(k, j, j % 3, to_plane(o, here), here).wait_send()

    def send_piece(j):
        t = j % 3
        here = turned(t)
        for n, o in enumerate(COLUMN):
            dev = from_column(o, here)
            column_copy(n, j, t, dev, dev[2] * 2 + dev[3]).wait_recv()

        @pl.when(j >= 2)
        def _():
            sent(j - 2)

        step = ALL // 8

        def tile(i, carry):
            rows = pl.ds(pl.multiple_of(i * step, 16), step)
            stage[j % 2, rows, :] = jnp.dot(select[t, rows, :], x_all[j], preferred_element_type=F32).astype(BF16)
            return carry

        lax.fori_loop(0, 8, tile, 0)
        for k, o in enumerate(OFFSETS):
            message(k, j, t, to_plane(o, here), here).start()
        own_rows = pl.ds(pl.multiple_of(plane_index(here) * MSG, 16), MSG)
        own_place = pl.ds(pl.multiple_of((here[0] * 4 + here[1]) * MSG, 16), MSG)
        got[j, here[3], own_place, :] = stage[j % 2, own_rows, :]

    def use_piece(j):
        t = j % 3
        here = turned(t)
        for load in weight_loads(j):
            load.wait()
        for k, o in enumerate(OFFSETS):
            message(k, j, t, here, from_plane(o, here)).wait_recv()

        @pl.when(t == 0)
        def _():
            sorted_rows[...] = got[j]

        @pl.when(t == 1)
        def _():
            for half in range(2):
                for i in range(4):
                    rows = slice(i * 320, (i + 1) * 320)
                    sorted_rows[half, rows, :] = jnp.dot(
                        swap[...], got[j, half, rows, :], preferred_element_type=F32
                    ).astype(BF16)

        @pl.when(t == 2)
        def _():
            def tile(i, carry):
                rows = pl.ds(pl.multiple_of(i * 320, 16), 320)
                for half in range(2):
                    sorted_rows[half, rows, :] = jnp.dot(
                        turn[rows, :], got[j, half], preferred_element_type=F32
                    ).astype(BF16)
                return carry

            lax.fori_loop(0, 4, tile, 0)

        step = ROWS // 5

        def tile(i, carry):
            rows = pl.ds(pl.multiple_of(i * step, 16), step)
            left = sorted_rows[0, rows, :]
            right = sorted_rows[1, rows, :]
            for n in range(2):
                acc[n, rows, :] += jnp.dot(left, weights[j % 2, n, 0], preferred_element_type=F32) + jnp.dot(
                    right, weights[j % 2, n, 1], preferred_element_type=F32
                )
            return carry

        lax.fori_loop(0, 5, tile, 0)

        @pl.when(j + 2 < PIECES)
        def _():
            for load in weight_loads(j + 2):
                load.start()

    def step(j, carry):
        @pl.when(j < PIECES)
        def _():
            send_piece(j)

        @pl.when(j == 0)
        def _():
            acc[...] = jnp.zeros_like(acc)
            swap[...] = swap_matrix()

            def tile(i, inner):
                turn[pl.ds(pl.multiple_of(i * 64, 64), 64), :] = turn_matrix(64, i * 64, False)
                return inner

            lax.fori_loop(0, ROWS // 64, tile, 0)

        @pl.when(j < 2)
        def _():
            fill(j + 1)

        @pl.when(j >= 1)
        def _():
            use_piece(j - 1)

        return carry

    lax.fori_loop(0, PIECES + 1, step, 0)

    def finish(i, carry):
        rows = pl.ds(pl.multiple_of(i * MSG, 16), MSG)
        g = acc[0, rows, :]
        act[rows, :] = (g / (1.0 + jnp.exp(-g)) * acc[1, rows, :]).astype(BF16)
        return carry

    lax.fori_loop(0, ROWS // MSG, finish, 0)

    for j in (PIECES - 2, PIECES - 1):
        sent(j)

    def sent_columns(j, carry):
        here = turned(j % 3)
        for n, o in enumerate(COLUMN):
            column_copy(n, j, j % 3, to_column(o, here), here[2] * 2 + here[3]).wait_send()
        return carry

    lax.fori_loop(0, PIECES, sent_columns, 0)


def dispatch(normed, table, w_gate, w_up):
    vmem = pl.BlockSpec(memory_space=pltpu.VMEM)
    hbm = pl.BlockSpec(memory_space=pltpu.HBM)
    dma = pltpu.SemaphoreType.DMA
    return pl.pallas_call(
        dispatch_kernel,
        name="dispatch",
        out_shape=[
            jax.ShapeDtypeStruct((ROWS, FF), BF16),
            jax.ShapeDtypeStruct((TYPES, 8, 2, PLANE, TOK), F32),
        ],
        in_specs=[hbm] * 4,
        out_specs=[vmem] * 2,
        scratch_shapes=[
            pltpu.VMEM((TOK, D), BF16),
            pltpu.VMEM((TYPES, 4, 2, PLANE, TOK), BF16),
            pltpu.VMEM((PIECES, 8 * TOK, PIECE), BF16),
            pltpu.VMEM((TYPES, 8, 2, PLANE, TOK), BF16),
            pltpu.VMEM((TYPES, ALL, 8 * TOK), BF16),
            pltpu.VMEM((2, ALL, PIECE), BF16),
            pltpu.VMEM((PIECES, 2, ROWS, PIECE), BF16),
            pltpu.VMEM((2, 2, 2, PIECE, FF), BF16),
            pltpu.VMEM((2, ROWS, FF), F32),
            pltpu.VMEM((320, 320), BF16),
            pltpu.VMEM((ROWS, ROWS), BF16),
            pltpu.VMEM((2, ROWS, PIECE), BF16),
            dma((2,)),
            dma((2, 2, 2)),
            dma((TYPES, len(COLUMN))),
            dma((TYPES, len(COLUMN))),
            dma((PIECES, len(COLUMN))),
            dma((PIECES, len(COLUMN))),
            dma((PIECES, len(OFFSETS))),
            dma((PIECES, len(OFFSETS))),
        ],
        compiler_params=pltpu.CompilerParams(
            collective_id=2, has_side_effects=True, vmem_limit_bytes=60 * 2**20
        ),
    )(normed, table, w_gate, w_up)


def combine_kernel(
    act_hbm, tables_hbm, w_down, hidden_hbm, out,
    acts, tables, wd, hidden, answers, got, mix, partial, sums, swap, turn,
    in_sem, msg_s, msg_r, col_s, col_r,
):
    loads = [
        pltpu.make_async_copy(act_hbm, acts.at[0], in_sem.at[0]),
        pltpu.make_async_copy(w_down, wd, in_sem.at[1]),
        pltpu.make_async_copy(tables_hbm, tables, in_sem.at[2]),
        pltpu.make_async_copy(hidden_hbm, hidden, in_sem.at[3]),
    ]
    for load in loads:
        load.start()
    greet_all()
    for load in loads:
        load.wait()

    def message(k, j, t, dev, src_dev):
        chip = dev[0] * 4 + dev[1]
        return pltpu.make_async_remote_copy(
            src_ref=answers.at[j % 3, dev[3], pl.ds(pl.multiple_of(chip * MSG, 16), MSG)],
            dst_ref=got.at[j, pl.ds(pl.multiple_of(plane_index(src_dev) * MSG, 16), MSG)],
            send_sem=msg_s.at[j, k], recv_sem=msg_r.at[j, k],
            device_id=turned_device(t, dev), device_id_type=MESH,
        )

    def column_copy(n, j, t, dev, src_dev):
        block = dev[2] * 2 + dev[3]
        return pltpu.make_async_remote_copy(
            src_ref=partial.at[j % 2, pl.ds(pl.multiple_of(block * TOK, TOK), TOK)],
            dst_ref=sums.at[j, src_dev[2], src_dev[3]],
            send_sem=col_s.at[j, n], recv_sem=col_r.at[j, n],
            device_id=turned_device(t, dev), device_id_type=MESH,
        )

    def sent(j):
        here = turned(j % 3)
        for k, o in enumerate(OFFSETS):
            message(k, j, j % 3, to_plane(o, here), here).wait_send()

    def sent_columns(j):
        here = turned(j % 3)
        for n, o in enumerate(COLUMN):
            column_copy(n, j, j % 3, to_column(o, here), here).wait_send()

    def send_piece(j):
        t = j % 3
        here = turned(t)
        for half in range(2):
            span = pl.ds(pl.multiple_of(half * HALF + j * PIECE, PIECE), PIECE)

            def tile(i, inner):
                rows = pl.ds(pl.multiple_of(i * (ROWS // 4), 16), ROWS // 4)
                answers[j % 3, half, rows, :] = jnp.dot(
                    acts[t, rows, :], wd[:, span], preferred_element_type=F32
                ).astype(BF16)
                return inner

            lax.fori_loop(0, 4, tile, 0)
        for k, o in enumerate(OFFSETS):
            message(k, j, t, to_plane(o, here), here).start()
        own_rows = pl.ds(pl.multiple_of(plane_index(here) * MSG, 16), MSG)
        own_place = pl.ds(pl.multiple_of((here[0] * 4 + here[1]) * MSG, 16), MSG)
        got[j, own_rows, :] = answers[j % 3, here[3], own_place, :]

    send_piece(0)
    swap[...] = swap_matrix()
    for i in range(4):
        rows = slice(i * 320, (i + 1) * 320)
        acts[1, rows, :] = jnp.dot(swap[...], acts[0, rows, :], preferred_element_type=F32).astype(BF16)
    send_piece(1)

    def turn_rows(i, carry):
        turn[...] = turn_matrix(64, i * 64, True)
        acts[2, pl.ds(pl.multiple_of(i * 64, 64), 64), :] = jnp.dot(
            turn[...], acts[0], preferred_element_type=F32
        ).astype(BF16)
        return carry

    lax.fori_loop(0, ROWS // 64, turn_rows, 0)
    send_piece(2)

    block, place = table_rows()

    def fill(i, carry):
        t = i // 4
        p = i % 4
        for b in range(8):
            rows = []
            for n in range(8):
                l = p * 8 + n
                hit = (tables[t, b, 0, pl.ds(l, 1), :] == place) & (block == b)
                rows.append(jnp.where(hit, tables[t, b, 1, pl.ds(l, 1), :], 0.0))
            whole = jnp.concatenate(rows, axis=0)
            mix[t, b * TOK : (b + 1) * TOK, pl.ds(pl.multiple_of(p * 8 * MSG, TOK), 8 * MSG)] = whole.T.astype(BF16)
        return carry

    lax.fori_loop(0, TYPES * PLANE // 8, fill, 0)

    def reduce_piece(j):
        t = j % 3
        here = turned(t)
        for k, o in enumerate(OFFSETS):
            message(k, j, t, here, from_plane(o, here)).wait_recv()

        @pl.when(j >= 2)
        def _():
            sent_columns(j - 2)

        def tile(i, carry):
            rows = pl.ds(pl.multiple_of(i * 256, 256), 256)
            partial[j % 2, rows, :] = jnp.dot(mix[t, rows, :], got[j], preferred_element_type=F32).astype(BF16)
            return carry

        lax.fori_loop(0, 4, tile, 0)
        for n, o in enumerate(COLUMN):
            column_copy(n, j, t, to_column(o, here), here).start()
        me = here[2] * 2 + here[3]
        sums[j, here[2], here[3]] = partial[j % 2, pl.ds(pl.multiple_of(me * TOK, TOK), TOK), :]

    def finish_piece(j):
        t = j % 3
        here = turned(t)
        for n, o in enumerate(COLUMN):
            column_copy(n, j, t, here, from_column(o, here)).wait_recv()
        for half in range(2):
            span = pl.ds(pl.multiple_of(half * HALF + j * PIECE, PIECE), PIECE)
            total = hidden[:, span]
            for n in range(4):
                total = total + sums[j, n, half].astype(F32)
            out[:, span] = total.astype(BF16)

    def step(j, carry):
        @pl.when(j < PIECES)
        def _():
            reduce_piece(j)

        @pl.when(j < PIECES - 3)
        def _():
            sent(j)
            send_piece(j + 3)

        @pl.when(j >= 1)
        def _():
            finish_piece(j - 1)

        return carry

    lax.fori_loop(0, PIECES + 1, step, 0)

    for j in range(PIECES - 3, PIECES):
        sent(j)
    for j in range(PIECES - 2, PIECES):
        sent_columns(j)


def combine(act, tables, w_down, hidden):
    hbm = pl.BlockSpec(memory_space=pltpu.HBM)
    dma = pltpu.SemaphoreType.DMA
    return pl.pallas_call(
        combine_kernel,
        name="combine",
        out_shape=jax.ShapeDtypeStruct((TOK, D), BF16),
        in_specs=[hbm] * 4,
        out_specs=pl.BlockSpec(memory_space=pltpu.VMEM),
        scratch_shapes=[
            pltpu.VMEM((TYPES, ROWS, FF), BF16),
            pltpu.VMEM((TYPES, 8, 2, PLANE, TOK), F32),
            pltpu.VMEM((FF, D), BF16),
            pltpu.VMEM((TOK, D), F32),
            pltpu.VMEM((3, 2, ROWS, PIECE), BF16),
            pltpu.VMEM((PIECES, ALL, PIECE), BF16),
            pltpu.VMEM((TYPES, 8 * TOK, ALL), BF16),
            pltpu.VMEM((2, 8 * TOK, PIECE), BF16),
            pltpu.VMEM((PIECES, 4, 2, TOK, PIECE), BF16),
            pltpu.VMEM((320, 320), BF16),
            pltpu.VMEM((64, ROWS), BF16),
            dma((4,)),
            dma((PIECES, len(OFFSETS))),
            dma((PIECES, len(OFFSETS))),
            dma((PIECES, len(COLUMN))),
            dma((PIECES, len(COLUMN))),
        ],
        compiler_params=pltpu.CompilerParams(
            collective_id=3, has_side_effects=True, vmem_limit_bytes=60 * 2**20
        ),
    )(act, tables, w_down, hidden)


def body(
    queries, fresh_keys, fresh_values, stored_keys, stored_values, column_blocks, diagonal_offsets,
    residual, norm_gain, routes, gate_weights, w_gate, w_up, w_down,
):
    kv = exchange(*collect(column_blocks, diagonal_offsets, stored_keys, stored_values))
    hidden, normed, table = attend(
        column_blocks, diagonal_offsets, queries, fresh_keys, fresh_values, kv,
        residual, norm_gain, routes, gate_weights,
    )
    act, tables = dispatch(normed, table, w_gate[0], w_up[0])
    return combine(act, tables, w_down[0], hidden)


def solution(mesh):
    rows = P(("ctx", "exp"), None)
    experts = P(("ctx", "exp"), None, None)
    in_specs = (
        rows, rows, rows, P("ctx", None), P("ctx", None), P(), P(), rows, P(), rows, rows,
        experts, experts, experts,
    )
    return jax.shard_map(body, mesh=mesh, in_specs=in_specs, out_specs=rows, check_vma=False)
```

time: 346 us -> 322 us (0.931); the launches traced: 346 us -> 318 us
  Pallas kernels: 335 us -> 309 us
    pallas_call x1, Pallas kernels: 157 us -> 129 us  [combine(): pl.pallas_call(combine_kernel, name='combine', out_shape=jax.ShapeDtypeSt...]
    pallas_call x1, Pallas kernels: 154 us -> 161 us  [dispatch(): pl.pallas_call(dispatch_kernel, name='dispatch', out_shape=[jax.ShapeDtyp...]
    pallas_call x1, Pallas kernels: 16.5 us -> 10.2 us  [exchange(): pl.pallas_call(exchange_kernel, name='key_exchange', out_shape=jax.ShapeD...]
where the time goes in v2:
time: 322 us; the launch traced here: 318 us
  Pallas kernels  309 us (96%)
  local copies, waits for them, and re-layouts  9.1 us (3%)
    pallas_call x1, Pallas kernels, dispatch(): pl.pallas_call(dispatch_kernel, name='dispatch', out_shape=[jax.ShapeDtyp...  161 us
    pallas_call x1, Pallas kernels, combine(): pl.pallas_call(combine_kernel, name='combine', out_shape=jax.ShapeDtypeSt...  129 us
    pallas_call x1, Pallas kernels, exchange(): pl.pallas_call(exchange_kernel, name='key_exchange', out_shape=jax.ShapeD...  10.2 us
    unnamed x33, local copies, waits for them, and re-layouts  9.1 us
    pallas_call x1, Pallas kernels, attend(): pl.pallas_call(attend_kernel, name='attention', out_shape=[jax.ShapeDtype...  7.94 us

profile of v2, /device:TPU:5, one launch (start us, length us, event | category | flops | bytes accessed | tf_op | source)
XLA Modules:
  0.0 318.4 jit_solution(12494933128616808700)
XLA Ops:
  0.0 0.0 copy-start.3
  0.0 1.2 copy-done.3
  1.2 0.0 copy-start.4
  1.2 1.2 copy-done.4
  2.5 0.0 copy-start.10
  2.5 0.7 copy-done.10
  3.1 0.0 copy-start.12
  3.1 0.7 copy-done.12
  3.8 0.0 copy-start.9
  3.8 0.0 copy-start.11
  3.8 0.0 copy-start.13
  3.9 0.0 copy-start.14
  3.9 0.0 copy-start.15
  3.9 1.1 collect_blocks.1
  5.0 10.2 %key_exchange.1.kv = bf16[2,2,1152,128]{3,2,1,0:T(8,128)(2,1)S(1)} custom-call(bf16[2,2,1152,128]{3,2,1,0:T(8,128)(2,1)S(1)} %get-tuple-element.12.con, f32[36,8,128]{2,1,0:T(8,128)S(1)} %get-tuple-element.13.near), custom_call_target="tpu_custom_call" | custom-call | tf_op jit(solution)/shard_map/key_exchange/pallas_call | solution.py:313
  15.2 0.0 copy-done.1
  15.2 0.0 copy-done.2
  15.2 0.0 copy-done.7
  15.2 0.0 copy-done.8
  15.2 0.0 copy-done.9
  15.2 0.0 copy-done.11
  15.3 0.0 copy-done.13
  15.3 0.0 copy-done.14
  15.3 0.0 copy-done.15
  15.3 7.9 %attention.1 = (f32[128,4096]{1,0:T(8,128)S(1)}, bf16[128,4096]{1,0:T(8,128)(2,1)S(1)}, bf16[3,4,2,32,128]{4,3,2,1,0:T(8,128)(2,1)S(1)}) custom-call(s32[2,2]{1,0:T(2,128)S(1)} %copy-done.11, s32[2,8]{1,0:T(2,128)S(1)} %copy-done.13, bf16[128,4096]{1,0:T(8,128)(2,1)S(1)} %copy-done.1, bf16[128,256]{1,0:T(8,128)(2,1)S(1)} %copy-done.7, ...), custom_call_target="tpu_custom_call" | custom-call | tf_op jit(solution)/shard_map/attention/pallas_call | solution.py:424
  23.2 0.0 copy-start
  23.2 1.3 copy-done
  24.6 1.0 copy-done.5
  25.5 0.7 copy-done.6
  26.2 161.1 %dispatch.1 = (bf16[1280,768]{1,0:T(8,128)(2,1)}, f32[3,8,2,32,128]{4,3,2,1,0:T(8,128)}) custom-call(bf16[128,4096]{1,0:T(8,128)(2,1)} %copy-done.5, bf16[3,4,2,32,128]{4,3,2,1,0:T(8,128)(2,1)} %copy-done.6, bf16[4096,768]{1,0:T(8,128)(2,1)} %bitcast.10, bf16[4096,768]{1,0:T(8,128)(2,1)} %bitcast.11), custom_call_target="tpu_custom_call" | custom-call | tf_op jit(solution)/shard_map/dispatch/pallas_call | solution.py:673
  187.4 128.7 %combine.1 = bf16[128,4096]{1,0:T(8,128)(2,1)} custom-call(bf16[1280,768]{1,0:T(8,128)(2,1)} %get-tuple-element.16.act_hbm, f32[3,8,2,32,128]{4,3,2,1,0:T(8,128)} %get-tuple-element.17.tables_hbm, bf16[768,4096]{1,0:T(8,128)(2,1)} %bitcast.9, f32[128,4096]{1,0:T(8,128)} %copy-done), custom_call_target="tpu_custom_call" | custom-call | tf_op jit(solution)/shard_map/combine/pallas_call | solution.py:869
  316.1 2.3 copy.16
  (6 shorter events, 0.0 us)
Async XLA Ops:
  0.0 1.2 copy-start.3
  1.2 1.2 copy-start.4
  2.5 0.7 copy-start.10
  3.1 0.7 copy-start.12
  3.8 11.4 %copy-start.1 = (bf16[128,4096]{1,0:T(8,128)(2,1)S(1)}, bf16[128,4096]{1,0:T(8,128)(2,1)}, u32[]{:S(2)}) copy-start(bf16[128,4096]{1,0:T(8,128)(2,1)} %q.1) | copy-start | bytes 3145732
  3.8 11.4 %copy-start.2 = (bf16[128,4096]{1,0:T(8,128)(2,1)S(1)}, bf16[128,4096]{1,0:T(8,128)(2,1)}, u32[]{:S(2)}) copy-start(bf16[128,4096]{1,0:T(8,128)(2,1)} %res.1) | copy-start | bytes 3145732
  3.8 11.4 %copy-start.7 = (bf16[128,256]{1,0:T(8,128)(2,1)S(1)}, bf16[128,256]{1,0:T(8,128)(2,1)}, u32[]{:S(2)}) copy-start(bf16[128,256]{1,0:T(8,128)(2,1)} %fk.1) | copy-start | bytes 196612
  3.8 11.4 %copy-start.8 = (bf16[128,256]{1,0:T(8,128)(2,1)S(1)}, bf16[128,256]{1,0:T(8,128)(2,1)}, u32[]{:S(2)}) copy-start(bf16[128,256]{1,0:T(8,128)(2,1)} %fv.1) | copy-start | bytes 196612
  3.8 11.4 %copy-start.9 = (f32[4096]{0:T(1024)S(1)}, f32[4096]{0:T(1024)}, u32[]{:S(2)}) copy-start(f32[4096]{0:T(1024)} %param.22) | copy-start | bytes 49156
  3.8 11.4 %copy-start.11 = (s32[2,2]{1,0:T(2,128)S(1)}, s32[2,2]{1,0:T(2,128)}, u32[]{:S(2)}) copy-start(s32[2,2]{1,0:T(2,128)} %cols.3) | copy-start | bytes 52
  3.8 11.4 %copy-start.13 = (s32[2,8]{1,0:T(2,128)S(1)}, s32[2,8]{1,0:T(2,128)}, u32[]{:S(2)}) copy-start(s32[2,8]{1,0:T(2,128)} %offs.3) | copy-start | bytes 196
  3.9 11.4 %copy-start.14 = (s32[128,8]{0,1:T(8,128)S(1)}, s32[128,8]{0,1:T(8,128)}, u32[]{:S(2)}) copy-start(s32[128,8]{0,1:T(8,128)} %param.23) | copy-start | bytes 12292
  3.9 11.4 %copy-start.15 = (f32[128,8]{0,1:T(8,128)S(1)}, f32[128,8]{0,1:T(8,128)}, u32[]{:S(2)}) copy-start(f32[128,8]{0,1:T(8,128)} %param.24) | copy-start | bytes 12292
  23.2 1.3 copy-start
  24.6 1.0 copy-start.5
  25.5 0.7 copy-start.6

commit v3 on v2

--- a/solution.py
+++ b/solution.py
@@ -31,6 +31,9 @@
 NEG = -1e30
 
 
+STAGED = 5
+AHEAD = 4
+ANSWERED = 4
 TYPES = 3
 
 
@@ -115,6 +118,29 @@
 
 def from_column(o, dev):
     return dev[0], dev[1], (dev[2] + 4 - o[0]) % 4, (dev[3] + 2 - o[1]) % 2
+
+
+CUTS = (0, 11, 21, 31)
+
+
+def roll(start, step):
+    kinds = [(step + 3 - i) % 3 for i in range(3)]
+    places = [turned(t) for t in kinds]
+    steady = (step >= 2) & (step < PIECES)
+
+    @pl.when(steady)
+    def _():
+        for n in range(CUTS[1]):
+            for i in range(3):
+                if CUTS[i] + n < CUTS[i + 1]:
+                    start(CUTS[i] + n, step - i, kinds[i], places[i])
+
+    for i in range(3):
+
+        @pl.when(jnp.logical_not(steady) & (step >= i) & (step - i < PIECES))
+        def _():
+            for k in range(CUTS[i], CUTS[i + 1]):
+                start(k, step - i, kinds[i], places[i])
 
 
 def greet_all():
@@ -530,7 +556,7 @@
     def message(k, j, t, dev, src_dev):
         chip = src_dev[0] * 4 + src_dev[1]
         return pltpu.make_async_remote_copy(
-            src_ref=stage.at[j % 2, pl.ds(pl.multiple_of(plane_index(dev) * MSG, 16), MSG)],
+            src_ref=stage.at[j % STAGED, pl.ds(pl.multiple_of(plane_index(dev) * MSG, 16), MSG)],
             dst_ref=got.at[j, src_dev[3], pl.ds(pl.multiple_of(chip * MSG, 16), MSG)],
             send_sem=msg_s.at[j, k], recv_sem=msg_r.at[j, k],
             device_id=turned_device(t, dev), device_id_type=MESH,
@@ -548,23 +574,24 @@
             dev = from_column(o, here)
             column_copy(n, j, t, dev, dev[2] * 2 + dev[3]).wait_recv()
 
-        @pl.when(j >= 2)
-        def _():
-            sent(j - 2)
+        @pl.when(j >= STAGED)
+        def _():
+            sent(j - STAGED)
 
         step = ALL // 8
 
         def tile(i, carry):
             rows = pl.ds(pl.multiple_of(i * step, 16), step)
-            stage[j % 2, rows, :] = jnp.dot(select[t, rows, :], x_all[j], preferred_element_type=F32).astype(BF16)
+            stage[j % STAGED, rows, :] = jnp.dot(select[t, rows, :], x_all[j], preferred_element_type=F32).astype(BF16)
             return carry
 
         lax.fori_loop(0, 8, tile, 0)
-        for k, o in enumerate(OFFSETS):
-            message(k, j, t, to_plane(o, here), here).start()
         own_rows = pl.ds(pl.multiple_of(plane_index(here) * MSG, 16), MSG)
         own_place = pl.ds(pl.multiple_of((here[0] * 4 + here[1]) * MSG, 16), MSG)
-        got[j, here[3], own_place, :] = stage[j % 2, own_rows, :]
+        got[j, here[3], own_place, :] = stage[j % STAGED, own_rows, :]
+
+    def start(k, j, t, here):
+        message(k, j, t, to_plane(OFFSETS[k], here), here).start()
 
     def use_piece(j):
         t = j % 3
@@ -591,9 +618,10 @@
         def _():
             def tile(i, carry):
                 rows = pl.ds(pl.multiple_of(i * 320, 16), 320)
+                turn[...] = turn_matrix(320, i * 320, False)
                 for half in range(2):
                     sorted_rows[half, rows, :] = jnp.dot(
-                        turn[rows, :], got[j, half], preferred_element_type=F32
+                        turn[...], got[j, half], preferred_element_type=F32
                     ).astype(BF16)
                 return carry
 
@@ -623,28 +651,24 @@
         def _():
             send_piece(j)
 
+        roll(start, j)
+
         @pl.when(j == 0)
         def _():
             acc[...] = jnp.zeros_like(acc)
             swap[...] = swap_matrix()
 
-            def tile(i, inner):
-                turn[pl.ds(pl.multiple_of(i * 64, 64), 64), :] = turn_matrix(64, i * 64, False)
-                return inner
-
-            lax.fori_loop(0, ROWS // 64, tile, 0)
-
         @pl.when(j < 2)
         def _():
             fill(j + 1)
 
-        @pl.when(j >= 1)
-        def _():
-            use_piece(j - 1)
+        @pl.when(j >= AHEAD)
+        def _():
+            use_piece(j - AHEAD)
 
         return carry
 
-    lax.fori_loop(0, PIECES + 1, step, 0)
+    lax.fori_loop(0, PIECES + AHEAD, step, 0)
 
     def finish(i, carry):
         rows = pl.ds(pl.multiple_of(i * MSG, 16), MSG)
@@ -654,7 +678,7 @@
 
     lax.fori_loop(0, ROWS // MSG, finish, 0)
 
-    for j in (PIECES - 2, PIECES - 1):
+    for j in range(PIECES - STAGED, PIECES):
         sent(j)
 
     def sent_columns(j, carry):
@@ -685,12 +709,12 @@
             pltpu.VMEM((PIECES, 8 * TOK, PIECE), BF16),
             pltpu.VMEM((TYPES, 8, 2, PLANE, TOK), BF16),
             pltpu.VMEM((TYPES, ALL, 8 * TOK), BF16),
-            pltpu.VMEM((2, ALL, PIECE), BF16),
+            pltpu.VMEM((STAGED, ALL, PIECE), BF16),
             pltpu.VMEM((PIECES, 2, ROWS, PIECE), BF16),
             pltpu.VMEM((2, 2, 2, PIECE, FF), BF16),
             pltpu.VMEM((2, ROWS, FF), F32),
             pltpu.VMEM((320, 320), BF16),
-            pltpu.VMEM((ROWS, ROWS), BF16),
+            pltpu.VMEM((320, ROWS), BF16),
             pltpu.VMEM((2, ROWS, PIECE), BF16),
             dma((2,)),
             dma((2, 2, 2)),
@@ -702,7 +726,7 @@
             dma((PIECES, len(OFFSETS))),
         ],
         compiler_params=pltpu.CompilerParams(
-            collective_id=2, has_side_effects=True, vmem_limit_bytes=60 * 2**20
+            collective_id=2, has_side_effects=True, vmem_limit_bytes=62 * 2**20
         ),
     )(normed, table, w_gate, w_up)
 
@@ -727,7 +751,7 @@
     def message(k, j, t, dev, src_dev):
         chip = dev[0] * 4 + dev[1]
         return pltpu.make_async_remote_copy(
-            src_ref=answers.at[j % 3, dev[3], pl.ds(pl.multiple_of(chip * MSG, 16), MSG)],
+            src_ref=answers.at[j % ANSWERED, dev[3], pl.ds(pl.multiple_of(chip * MSG, 16), MSG)],
             dst_ref=got.at[j, pl.ds(pl.multiple_of(plane_index(src_dev) * MSG, 16), MSG)],
             send_sem=msg_s.at[j, k], recv_sem=msg_r.at[j, k],
             device_id=turned_device(t, dev), device_id_type=MESH,
@@ -760,17 +784,17 @@
 
             def tile(i, inner):
                 rows = pl.ds(pl.multiple_of(i * (ROWS // 4), 16), ROWS // 4)
-                answers[j % 3, half, rows, :] = jnp.dot(
+                answers[j % ANSWERED, half, rows, :] = jnp.dot(
                     acts[t, rows, :], wd[:, span], preferred_element_type=F32
                 ).astype(BF16)
                 return inner
 
             lax.fori_loop(0, 4, tile, 0)
+        own_rows = pl.ds(pl.multiple_of(plane_index(here) * MSG, 16), MSG)
+        own_place = pl.ds(pl.multiple_of((here[0] * 4 + here[1]) * MSG, 16), MSG)
+        got[j, own_rows, :] = answers[j % ANSWERED, here[3], own_place, :]
         for k, o in enumerate(OFFSETS):
             message(k, j, t, to_plane(o, here), here).start()
-        own_rows = pl.ds(pl.multiple_of(plane_index(here) * MSG, 16), MSG)
-        own_place = pl.ds(pl.multiple_of((here[0] * 4 + here[1]) * MSG, 16), MSG)
-        got[j, own_rows, :] = answers[j % 3, here[3], own_place, :]
 
     send_piece(0)
     swap[...] = swap_matrix()
@@ -787,7 +811,12 @@
         return carry
 
     lax.fori_loop(0, ROWS // 64, turn_rows, 0)
-    send_piece(2)
+
+    def send_more(j, carry):
+        send_piece(j)
+        return carry
+
+    lax.fori_loop(2, ANSWERED, send_more, 0)
 
     block, place = table_rows()
 
@@ -844,10 +873,10 @@
         def _():
             reduce_piece(j)
 
-        @pl.when(j < PIECES - 3)
+        @pl.when(j < PIECES - ANSWERED)
         def _():
             sent(j)
-            send_piece(j + 3)
+            send_piece(j + ANSWERED)
 
         @pl.when(j >= 1)
         def _():
@@ -857,7 +886,7 @@
 
     lax.fori_loop(0, PIECES + 1, step, 0)
 
-    for j in range(PIECES - 3, PIECES):
+    for j in range(PIECES - ANSWERED, PIECES):
         sent(j)
     for j in range(PIECES - 2, PIECES):
         sent_columns(j)
@@ -877,7 +906,7 @@
             pltpu.VMEM((TYPES, 8, 2, PLANE, TOK), F32),
             pltpu.VMEM((FF, D), BF16),
             pltpu.VMEM((TOK, D), F32),
-            pltpu.VMEM((3, 2, ROWS, PIECE), BF16),
+            pltpu.VMEM((ANSWERED, 2, ROWS, PIECE), BF16),
             pltpu.VMEM((PIECES, ALL, PIECE), BF16),
             pltpu.VMEM((TYPES, 8 * TOK, ALL), BF16),
             pltpu.VMEM((2, 8 * TOK, PIECE), BF16),
@@ -891,7 +920,7 @@
             dma((PIECES, len(COLUMN))),
         ],
         compiler_params=pltpu.CompilerParams(
-            collective_id=3, has_side_effects=True, vmem_limit_bytes=60 * 2**20
+            collective_id=3, has_side_effects=True, vmem_limit_bytes=62 * 2**20
         ),
     )(act, tables, w_down, hidden)
 

time: 322 us -> 295 us (0.916)
  Pallas kernels: 309 us -> 281 us
    pallas_call x1, Pallas kernels: 161 us -> 131 us  [dispatch(): pl.pallas_call(dispatch_kernel, name='dispatch', out_shape=[jax.ShapeDtyp...]
where the time goes in v3:
time: 295 us; the launch traced here: 290 us
  Pallas kernels  281 us (95%)
  local copies, waits for them, and re-layouts  9.1 us (3%)
    pallas_call x1, Pallas kernels, dispatch(): pl.pallas_call(dispatch_kernel, name='dispatch', out_shape=[jax.ShapeDtyp...  131 us
    pallas_call x1, Pallas kernels, combine(): pl.pallas_call(combine_kernel, name='combine', out_shape=jax.ShapeDtypeSt...  130 us
    pallas_call x1, Pallas kernels, exchange(): pl.pallas_call(exchange_kernel, name='key_exchange', out_shape=jax.ShapeD...  10.2 us
    unnamed x33, local copies, waits for them, and re-layouts  9.1 us
    pallas_call x1, Pallas kernels, attend(): pl.pallas_call(attend_kernel, name='attention', out_shape=[jax.ShapeDtype...  7.94 us

profile of v3, /device:TPU:5, one launch (start us, length us, event | category | flops | bytes accessed | tf_op | source)
XLA Modules:
  0.0 290.1 jit_solution(4278759490170002415)
XLA Ops:
  0.0 0.0 copy-start.3
  0.0 1.2 copy-done.3
  1.2 0.0 copy-start.4
  1.2 1.2 copy-done.4
  2.5 0.0 copy-start.10
  2.5 0.7 copy-done.10
  3.1 0.0 copy-start.12
  3.1 0.7 copy-done.12
  3.8 0.0 copy-start.9
  3.8 0.0 copy-start.11
  3.8 0.0 copy-start.13
  3.9 0.0 copy-start.14
  3.9 0.0 copy-start.15
  3.9 1.1 collect_blocks.1
  5.0 10.2 %key_exchange.1.kv = bf16[2,2,1152,128]{3,2,1,0:T(8,128)(2,1)S(1)} custom-call(bf16[2,2,1152,128]{3,2,1,0:T(8,128)(2,1)S(1)} %get-tuple-element.12.con, f32[36,8,128]{2,1,0:T(8,128)S(1)} %get-tuple-element.13.near), custom_call_target="tpu_custom_call" | custom-call | tf_op jit(solution)/shard_map/key_exchange/pallas_call | solution.py:339
  15.2 0.0 copy-done.1
  15.2 0.0 copy-done.2
  15.2 0.0 copy-done.7
  15.2 0.0 copy-done.8
  15.2 0.0 copy-done.9
  15.2 0.0 copy-done.11
  15.3 0.0 copy-done.13
  15.3 0.0 copy-done.14
  15.3 0.0 copy-done.15
  15.3 7.9 %attention.1 = (f32[128,4096]{1,0:T(8,128)S(1)}, bf16[128,4096]{1,0:T(8,128)(2,1)S(1)}, bf16[3,4,2,32,128]{4,3,2,1,0:T(8,128)(2,1)S(1)}) custom-call(s32[2,2]{1,0:T(2,128)S(1)} %copy-done.11, s32[2,8]{1,0:T(2,128)S(1)} %copy-done.13, bf16[128,4096]{1,0:T(8,128)(2,1)S(1)} %copy-done.1, bf16[128,256]{1,0:T(8,128)(2,1)S(1)} %copy-done.7, ...), custom_call_target="tpu_custom_call" | custom-call | tf_op jit(solution)/shard_map/attention/pallas_call | solution.py:450
  23.2 0.0 copy-start
  23.2 1.3 copy-done
  24.6 1.0 copy-done.5
  25.5 0.7 copy-done.6
  26.2 131.3 %dispatch.1 = (bf16[1280,768]{1,0:T(8,128)(2,1)}, f32[3,8,2,32,128]{4,3,2,1,0:T(8,128)}) custom-call(bf16[128,4096]{1,0:T(8,128)(2,1)} %copy-done.5, bf16[3,4,2,32,128]{4,3,2,1,0:T(8,128)(2,1)} %copy-done.6, bf16[4096,768]{1,0:T(8,128)(2,1)} %bitcast.10, bf16[4096,768]{1,0:T(8,128)(2,1)} %bitcast.11), custom_call_target="tpu_custom_call" | custom-call | tf_op jit(solution)/shard_map/dispatch/pallas_call | solution.py:697
  157.6 130.3 %combine.1 = bf16[128,4096]{1,0:T(8,128)(2,1)} custom-call(bf16[1280,768]{1,0:T(8,128)(2,1)} %get-tuple-element.16.act_hbm, f32[3,8,2,32,128]{4,3,2,1,0:T(8,128)} %get-tuple-element.17.tables_hbm, bf16[768,4096]{1,0:T(8,128)(2,1)} %bitcast.9, f32[128,4096]{1,0:T(8,128)} %copy-done), custom_call_target="tpu_custom_call" | custom-call | tf_op jit(solution)/shard_map/combine/pallas_call | solution.py:898
  287.8 2.3 copy.16
  (6 shorter events, 0.0 us)
Async XLA Ops:
  0.0 1.2 copy-start.3
  1.2 1.2 copy-start.4
  2.5 0.7 copy-start.10
  3.1 0.7 copy-start.12
  3.8 11.4 %copy-start.1 = (bf16[128,4096]{1,0:T(8,128)(2,1)S(1)}, bf16[128,4096]{1,0:T(8,128)(2,1)}, u32[]{:S(2)}) copy-start(bf16[128,4096]{1,0:T(8,128)(2,1)} %q.1) | copy-start | bytes 3145732
  3.8 11.4 %copy-start.2 = (bf16[128,4096]{1,0:T(8,128)(2,1)S(1)}, bf16[128,4096]{1,0:T(8,128)(2,1)}, u32[]{:S(2)}) copy-start(bf16[128,4096]{1,0:T(8,128)(2,1)} %res.1) | copy-start | bytes 3145732
  3.8 11.4 %copy-start.7 = (bf16[128,256]{1,0:T(8,128)(2,1)S(1)}, bf16[128,256]{1,0:T(8,128)(2,1)}, u32[]{:S(2)}) copy-start(bf16[128,256]{1,0:T(8,128)(2,1)} %fk.1) | copy-start | bytes 196612
  3.8 11.4 %copy-start.8 = (bf16[128,256]{1,0:T(8,128)(2,1)S(1)}, bf16[128,256]{1,0:T(8,128)(2,1)}, u32[]{:S(2)}) copy-start(bf16[128,256]{1,0:T(8,128)(2,1)} %fv.1) | copy-start | bytes 196612
  3.8 11.4 %copy-start.9 = (f32[4096]{0:T(1024)S(1)}, f32[4096]{0:T(1024)}, u32[]{:S(2)}) copy-start(f32[4096]{0:T(1024)} %param.22) | copy-start | bytes 49156
  3.8 11.4 %copy-start.11 = (s32[2,2]{1,0:T(2,128)S(1)}, s32[2,2]{1,0:T(2,128)}, u32[]{:S(2)}) copy-start(s32[2,2]{1,0:T(2,128)} %cols.3) | copy-start | bytes 52
  3.8 11.4 %copy-start.13 = (s32[2,8]{1,0:T(2,128)S(1)}, s32[2,8]{1,0:T(2,128)}, u32[]{:S(2)}) copy-start(s32[2,8]{1,0:T(2,128)} %offs.3) | copy-start | bytes 196
  3.9 11.4 %copy-start.14 = (s32[128,8]{0,1:T(8,128)S(1)}, s32[128,8]{0,1:T(8,128)}, u32[]{:S(2)}) copy-start(s32[128,8]{0,1:T(8,128)} %param.23) | copy-start | bytes 12292
  3.9 11.4 %copy-start.15 = (f32[128,8]{0,1:T(8,128)S(1)}, f32[128,8]{0,1:T(8,128)}, u32[]{:S(2)}) copy-start(f32[128,8]{0,1:T(8,128)} %param.24) | copy-start | bytes 12292
  23.2 1.3 copy-start
  24.6 1.0 copy-start.5
  25.5 0.7 copy-start.6

commit v4 on v3

--- a/solution.py
+++ b/solution.py
@@ -33,6 +33,7 @@
 
 STAGED = 5
 AHEAD = 4
+BEHIND = 3
 ANSWERED = 4
 TYPES = 3
 
@@ -176,12 +177,24 @@
     return exp + h * (4 - 8 * ((exp // 4) % 2))
 
 
-def collect_kernel(cols, offs, keys_hbm, values_hbm, con, near, keys, values, sem):
+def collect_kernel(cols, offs, keys_hbm, values_hbm, con, near, bias_out, keys, values, sem):
     loads = [pltpu.make_async_copy(keys_hbm, keys, sem.at[0]), pltpu.make_async_copy(values_hbm, values, sem.at[1])]
     for load in loads:
         load.start()
     ctx = lax.axis_index("ctx")
     xl = ctx // 2
+    lane = lax.broadcasted_iota(jnp.int32, (8, (VERT + SLASH) * BLOCK), 1) // BLOCK
+    for h in range(HEADS_KV):
+        for i in range(2):
+            block = 128 + 2 * (ctx * 32 + lax.axis_index("exp")) + i
+            listed = [cols[h, v] for v in range(VERT)] + [block - offs[h, s] for s in range(SLASH)]
+            bias = jnp.zeros(lane.shape, F32)
+            for n, one in enumerate(listed):
+                kept = (one >= 0) & (one < 128)
+                for before in listed[:n]:
+                    kept = kept & (one != before)
+                bias = jnp.where(lane == n, jnp.where(kept, 0.0, NEG), bias)
+            bias_out[h * 2 + i] = bias
     for load in loads:
         load.wait()
 
@@ -217,19 +230,37 @@
         out_shape=[
             jax.ShapeDtypeStruct((2, HEADS_KV, SLOTS * BLOCK, HEAD), BF16),
             jax.ShapeDtypeStruct((HEADS_KV * SLOTS, 8, HEAD), F32),
+            jax.ShapeDtypeStruct((HEADS_KV * 2, 8, (VERT + SLASH) * BLOCK), F32),
         ],
         in_specs=[pl.BlockSpec(memory_space=pltpu.SMEM)] * 2 + [pl.BlockSpec(memory_space=pltpu.HBM)] * 2,
-        out_specs=[pl.BlockSpec(memory_space=pltpu.VMEM)] * 2,
+        out_specs=[pl.BlockSpec(memory_space=pltpu.VMEM)] * 3,
         scratch_shapes=[
             pltpu.VMEM((2048, HEADS_KV * HEAD), BF16),
             pltpu.VMEM((2048, HEADS_KV * HEAD), BF16),
             pltpu.SemaphoreType.DMA((2,)),
         ],
-        compiler_params=pltpu.CompilerParams(vmem_limit_bytes=16 * 2**20),
+        compiler_params=pltpu.CompilerParams(vmem_limit_bytes=60 * 2**20),
     )(cols, offs, keys, values)
 
 
-def exchange_kernel(con, near, out, sib, chip, rem, fin, arr, ssem, rsem):
+def front_kernel(
+    con_hbm, near_hbm, routes_hbm, gates_hbm, q_hbm, bias_hbm, fk_hbm, fv_hbm, res_hbm, gain_hbm,
+    hidden_out, normed_out, table_out,
+    con, near, routes, gates, q, bias_all, fk, fv, res, gain, hidden, normed, table,
+    out, sib, chip, rem, fin, arr, in_sem, sem, ssem, rsem,
+):
+    given = (con_hbm, near_hbm, routes_hbm, gates_hbm, q_hbm, bias_hbm, fk_hbm, fv_hbm, res_hbm, gain_hbm)
+    held = (con, near, routes, gates, q, bias_all, fk, fv, res, gain)
+    loads = [pltpu.make_async_copy(src, dst, in_sem.at[n]) for n, (src, dst) in enumerate(zip(given, held))]
+    for load in loads:
+        load.start()
+    puts = []
+
+    def put(src, dst):
+        copy = pltpu.make_async_copy(src, dst, sem.at[len(puts)])
+        copy.start()
+        puts.append(copy)
+
     x, y, z, c = coords()
     xl = x % 2
     exp = lax.axis_index("exp")
@@ -239,6 +270,8 @@
     for other in (twin, *across):
         pl.semaphore_signal(bar, inc=1, device_id=other, device_id_type=MESH)
     pl.semaphore_wait(bar, 3)
+    for load in loads[:2]:
+        load.wait()
 
     first = pltpu.make_async_remote_copy(
         src_ref=con.at[1 - c], dst_ref=sib, send_sem=ssem.at[0], recv_sem=rsem.at[0],
@@ -273,103 +306,8 @@
         for h in range(HEADS_KV):
             vertical(h).start()
 
-    def back(h):
-        return pltpu.make_async_remote_copy(
-            src_ref=fin.at[h], dst_ref=arr.at[h], send_sem=ssem.at[3 + h], recv_sem=rsem.at[3 + h],
-            device_id=twin, device_id_type=MESH,
-        )
-
-    def pick(h, slot):
-        span = slice(slot * BLOCK, (slot + 1) * BLOCK)
-        local = near[h * SLOTS + slot, 0:1, :].astype(BF16)
-        far = rem[h, span, :]
-        return span, chip[h, span, :] * local + far * (1.0 - local).astype(BF16), far
-
-    def pick_verticals(h):
-        for v in range(VERT):
-            span, mixed, _ = pick(h, v)
-            fin[h, span, :] = mixed
-            out[c, h, span, :] = mixed
-
-    for h in range(HEADS_KV):
-
-        @pl.when(xl == 0)
-        def _():
-            vertical(h).wait_recv()
-            pick_verticals(h)
-            fin[h, verts:, :] = jnp.zeros((2 * SLASH * BLOCK, HEAD), BF16)
-            out[c, h, verts:, :] = jnp.zeros((2 * SLASH * BLOCK, HEAD), BF16)
-
-        @pl.when(xl == 1)
-        def _():
-            whole(h).wait_recv()
-            pick_verticals(h)
-            for slot in range(VERT, SLOTS):
-                span, mixed, far = pick(h, slot)
-
-                @pl.when(c == 1)
-                def _():
-                    out[1, h, span, :] = mixed
-                    fin[h, span, :] = far
-
-                @pl.when(c == 0)
-                def _():
-                    out[0, h, span, :] = far
-                    fin[h, span, :] = mixed
-
-        back(h).start()
-
-    for h in range(HEADS_KV):
-        back(h).wait()
-        out[1 - c, h] = arr[h]
-
-    @pl.when(xl == 0)
-    def _():
-        for h in range(HEADS_KV):
-            whole(h).wait_send()
-
-    @pl.when(xl == 1)
-    def _():
-        for h in range(HEADS_KV):
-            vertical(h).wait_send()
-
-
-def exchange(con, near):
-    part = (HEADS_KV, SLOTS * BLOCK, HEAD)
-    return pl.pallas_call(
-        exchange_kernel,
-        name="key_exchange",
-        out_shape=jax.ShapeDtypeStruct((2,) + part, BF16),
-        in_specs=[pl.BlockSpec(memory_space=pltpu.VMEM)] * 2,
-        out_specs=pl.BlockSpec(memory_space=pltpu.VMEM),
-        scratch_shapes=[
-            pltpu.VMEM(part, BF16),
-            pltpu.VMEM(part, BF16),
-            pltpu.VMEM(part, BF16),
-            pltpu.VMEM(part, BF16),
-            pltpu.VMEM(part, BF16),
-            pltpu.SemaphoreType.DMA((5,)),
-            pltpu.SemaphoreType.DMA((5,)),
-        ],
-        compiler_params=pltpu.CompilerParams(
-            collective_id=1, has_side_effects=True, vmem_limit_bytes=24 * 2**20
-        ),
-    )(con, near)
-
-
-def attend_kernel(
-    cols, offs, q, fk, fv, kv, res, gain, routes, gates, hidden_out, normed_out, table_out,
-    hidden, normed, table, sem,
-):
-    puts = []
-
-    def put(src, dst):
-        copy = pltpu.make_async_copy(src, dst, sem.at[len(puts)])
-        copy.start()
-        puts.append(copy)
-
-    ctx = lax.axis_index("ctx")
-    exp = lax.axis_index("exp")
+    for load in loads[2:]:
+        load.wait()
 
     ids = routes[...]
     group, rest = ids >> 5, ids & 31
@@ -393,23 +331,75 @@
             table[t, n, 1] = strength[n * PLANE : (n + 1) * PLANE]
     put(table, table_out)
 
+    def back(h):
+        return pltpu.make_async_remote_copy(
+            src_ref=fin.at[h], dst_ref=arr.at[h], send_sem=ssem.at[3 + h], recv_sem=rsem.at[3 + h],
+            device_id=twin, device_id_type=MESH,
+        )
+
+    def pick(h, slot):
+        span = slice(slot * BLOCK, (slot + 1) * BLOCK)
+        local = near[h * SLOTS + slot, 0:1, :].astype(BF16)
+        far = rem[h, span, :]
+        return span, chip[h, span, :] * local + far * (1.0 - local).astype(BF16), far
+
+    def pick_verticals(h):
+        for v in range(VERT):
+            span, mixed, _ = pick(h, v)
+            fin[h, span, :] = mixed
+            out[c, h, span, :] = mixed
+
+    for h in range(HEADS_KV):
+
+        @pl.when(xl == 0)
+        def _():
+            vertical(h).wait_recv()
+            pick_verticals(h)
+            fin[h, verts:, :] = jnp.zeros((2 * SLASH * BLOCK, HEAD), BF16)
+            out[c, h, verts:, :] = jnp.zeros((2 * SLASH * BLOCK, HEAD), BF16)
+
+        @pl.when(xl == 1)
+        def _():
+            whole(h).wait_recv()
+            pick_verticals(h)
+            for slot in range(VERT, SLOTS):
+                span, mixed, far = pick(h, slot)
+
+                @pl.when(c == 1)
+                def _():
+                    out[1, h, span, :] = mixed
+                    fin[h, span, :] = far
+
+                @pl.when(c == 0)
+                def _():
+                    out[0, h, span, :] = far
+                    fin[h, span, :] = mixed
+
+        back(h).start()
+
+    for h in range(HEADS_KV):
+        back(h).wait()
+        out[1 - c, h] = arr[h]
+
+    @pl.when(xl == 0)
+    def _():
+        for h in range(HEADS_KV):
+            whole(h).wait_send()
+
+    @pl.when(xl == 1)
+    def _():
+        for h in range(HEADS_KV):
+            vertical(h).wait_send()
+
     scale = 1.0 / HEAD**0.5
-    lane = lax.broadcasted_iota(jnp.int32, (1, (VERT + SLASH) * BLOCK), 1) // BLOCK
     heads = 4
     ones = jnp.ones(((VERT + SLASH) * BLOCK, HEAD), BF16)
     for h in range(HEADS_KV):
         for i in range(2):
-            block = 128 + 2 * (ctx * 32 + exp) + i
-            listed = [cols[h, v] for v in range(VERT)] + [block - offs[h, s] for s in range(SLASH)]
-            bias = jnp.zeros(lane.shape, F32)
-            for n, one in enumerate(listed):
-                kept = (one >= 0) & (one < 128)
-                for before in listed[:n]:
-                    kept = kept & (one != before)
-                bias = jnp.where(lane == n, jnp.where(kept, 0.0, NEG), bias)
+            bias = bias_all[h * 2 + i, 0:1, :]
             slash = VERT * BLOCK + i * SLASH * BLOCK
-            k = jnp.concatenate([kv[0, h, : VERT * BLOCK, :], kv[0, h, slash : slash + SLASH * BLOCK, :]], axis=0)
-            v = jnp.concatenate([kv[1, h, : VERT * BLOCK, :], kv[1, h, slash : slash + SLASH * BLOCK, :]], axis=0)
+            k = jnp.concatenate([out[0, h, : VERT * BLOCK, :], out[0, h, slash : slash + SLASH * BLOCK, :]], axis=0)
+            v = jnp.concatenate([out[1, h, : VERT * BLOCK, :], out[1, h, slash : slash + SLASH * BLOCK, :]], axis=0)
             v = jnp.concatenate([v, ones], axis=1)
             rows = slice(i * BLOCK, (i + 1) * BLOCK)
             own_k = fk[rows, h * HEAD : (h + 1) * HEAD].astype(F32)
@@ -444,18 +434,31 @@
         copy.wait()
 
 
-def attend(cols, offs, q, fk, fv, kv, res, gain, routes, gates):
-    vmem = pl.BlockSpec(memory_space=pltpu.VMEM)
+def front(con, near, bias, q, fk, fv, res, gain, routes, gates):
+    part = (HEADS_KV, SLOTS * BLOCK, HEAD)
+    hbm = pl.BlockSpec(memory_space=pltpu.HBM)
+    args = (con, near, routes.T, gates.T, q, bias, fk, fv, res, gain.reshape(1, D))
     shapes = [((TOK, D), F32), ((TOK, D), BF16), ((TYPES, 4, 2, PLANE, TOK), BF16)]
     return pl.pallas_call(
-        attend_kernel,
-        name="attention",
+        front_kernel,
+        name="exchange_and_attention",
         out_shape=[jax.ShapeDtypeStruct(*one) for one in shapes],
-        in_specs=[pl.BlockSpec(memory_space=pltpu.SMEM)] * 2 + [vmem] * 8,
-        out_specs=[pl.BlockSpec(memory_space=pltpu.HBM)] * 3,
-        scratch_shapes=[pltpu.VMEM(*one) for one in shapes] + [pltpu.SemaphoreType.DMA((6,))],
-        compiler_params=pltpu.CompilerParams(vmem_limit_bytes=32 * 2**20),
-    )(cols, offs, q, fk, fv, kv, res, gain.reshape(1, D), routes.T, gates.T)
+        in_specs=[hbm] * len(args),
+        out_specs=[hbm] * 3,
+        scratch_shapes=[pltpu.VMEM(one.shape, one.dtype) for one in args]
+        + [pltpu.VMEM(*one) for one in shapes]
+        + [pltpu.VMEM((2,) + part, BF16)]
+        + [pltpu.VMEM(part, BF16)] * 5
+        + [
+            pltpu.SemaphoreType.DMA((len(args),)),
+            pltpu.SemaphoreType.DMA((6,)),
+            pltpu.SemaphoreType.DMA((5,)),
+            pltpu.SemaphoreType.DMA((5,)),
+        ],
+        compiler_params=pltpu.CompilerParams(
+            collective_id=1, has_side_effects=True, vmem_limit_bytes=60 * 2**20
+        ),
+    )(*args)
 
 
 def table_rows():
@@ -745,7 +748,7 @@
     for load in loads:
         load.start()
     greet_all()
-    for load in loads:
+    for load in loads[:2]:
         load.wait()
 
     def message(k, j, t, dev, src_dev):
@@ -760,7 +763,7 @@
     def column_copy(n, j, t, dev, src_dev):
         block = dev[2] * 2 + dev[3]
         return pltpu.make_async_remote_copy(
-            src_ref=partial.at[j % 2, pl.ds(pl.multiple_of(block * TOK, TOK), TOK)],
+            src_ref=partial.at[j, pl.ds(pl.multiple_of(block * TOK, TOK), TOK)],
             dst_ref=sums.at[j, src_dev[2], src_dev[3]],
             send_sem=col_s.at[j, n], recv_sem=col_r.at[j, n],
             device_id=turned_device(t, dev), device_id_type=MESH,
@@ -818,6 +821,8 @@
 
     lax.fori_loop(2, ANSWERED, send_more, 0)
 
+    for load in loads[2:]:
+        load.wait()
     block, place = table_rows()
 
     def fill(i, carry):
@@ -841,20 +846,14 @@
         for k, o in enumerate(OFFSETS):
             message(k, j, t, here, from_plane(o, here)).wait_recv()
 
-        @pl.when(j >= 2)
-        def _():
-            sent_columns(j - 2)
-
-        def tile(i, carry):
-            rows = pl.ds(pl.multiple_of(i * 256, 256), 256)
-            partial[j % 2, rows, :] = jnp.dot(mix[t, rows, :], got[j], preferred_element_type=F32).astype(BF16)
-            return carry
-
-        lax.fori_loop(0, 4, tile, 0)
-        for n, o in enumerate(COLUMN):
-            column_copy(n, j, t, to_column(o, here), here).start()
+        for far in (2, 1, 3, 0):
+            rows = pl.ds(pl.multiple_of(((here[2] + far) % 4) * 2 * TOK, 2 * TOK), 2 * TOK)
+            partial[j, rows, :] = jnp.dot(mix[t, rows, :], got[j], preferred_element_type=F32).astype(BF16)
+            for n, o in enumerate(COLUMN):
+                if o[0] == far:
+                    column_copy(n, j, t, to_column(o, here), here).start()
         me = here[2] * 2 + here[3]
-        sums[j, here[2], here[3]] = partial[j % 2, pl.ds(pl.multiple_of(me * TOK, TOK), TOK), :]
+        sums[j, here[2], here[3]] = partial[j, pl.ds(pl.multiple_of(me * TOK, TOK), TOK), :]
 
     def finish_piece(j):
         t = j % 3
@@ -878,17 +877,17 @@
             sent(j)
             send_piece(j + ANSWERED)
 
-        @pl.when(j >= 1)
-        def _():
-            finish_piece(j - 1)
+        @pl.when(j >= BEHIND)
+        def _():
+            finish_piece(j - BEHIND)
 
         return carry
 
-    lax.fori_loop(0, PIECES + 1, step, 0)
+    lax.fori_loop(0, PIECES + BEHIND, step, 0)
 
     for j in range(PIECES - ANSWERED, PIECES):
         sent(j)
-    for j in range(PIECES - 2, PIECES):
+    for j in range(PIECES):
         sent_columns(j)
 
 
@@ -909,7 +908,7 @@
             pltpu.VMEM((ANSWERED, 2, ROWS, PIECE), BF16),
             pltpu.VMEM((PIECES, ALL, PIECE), BF16),
             pltpu.VMEM((TYPES, 8 * TOK, ALL), BF16),
-            pltpu.VMEM((2, 8 * TOK, PIECE), BF16),
+            pltpu.VMEM((PIECES, 8 * TOK, PIECE), BF16),
             pltpu.VMEM((PIECES, 4, 2, TOK, PIECE), BF16),
             pltpu.VMEM((320, 320), BF16),
             pltpu.VMEM((64, ROWS), BF16),
@@ -929,10 +928,9 @@
     queries, fresh_keys, fresh_values, stored_keys, stored_values, column_blocks, diagonal_offsets,
     residual, norm_gain, routes, gate_weights, w_gate, w_up, w_down,
 ):
-    kv = exchange(*collect(column_blocks, diagonal_offsets, stored_keys, stored_values))
-    hidden, normed, table = attend(
-        column_blocks, diagonal_offsets, queries, fresh_keys, fresh_values, kv,
-        residual, norm_gain, routes, gate_weights,
+    con, near, bias = collect(column_blocks, diagonal_offsets, stored_keys, stored_values)
+    hidden, normed, table = front(
+        con, near, bias, queries, fresh_keys, fresh_values, residual, norm_gain, routes, gate_weights
     )
     act, tables = dispatch(normed, table, w_gate[0], w_up[0])
     return combine(act, tables, w_down[0], hidden)

time: 295 us -> 284 us (0.963)
  local copies, waits for them, and re-layouts: 9.1 us -> 2.29 us
    unnamed x33 -> x1, local copies, waits for them, and re-layouts: 9.1 us -> 2.29 us
    pallas_call x1, Pallas kernels: 130 us -> 127 us  [combine(): pl.pallas_call(combine_kernel, name='combine', out_shape=jax.ShapeDtypeSt...]
    pallas_call x2 -> x1, Pallas kernels: 18.1 us -> 16.9 us  [front(): pl.pallas_call(front_kernel, name='exchange_and_attention', out_shape=[ja...]
where the time goes in v4:
time: 284 us; the launch traced here: 282 us
  Pallas kernels  279 us (98%)
    pallas_call x1, Pallas kernels, dispatch(): pl.pallas_call(dispatch_kernel, name='dispatch', out_shape=[jax.ShapeDtyp...  131 us
    pallas_call x1, Pallas kernels, combine(): pl.pallas_call(combine_kernel, name='combine', out_shape=jax.ShapeDtypeSt...  127 us
    pallas_call x1, Pallas kernels, front(): pl.pallas_call(front_kernel, name='exchange_and_attention', out_shape=[ja...  16.9 us

profile of v4, /device:TPU:5, one launch (start us, length us, event | category | flops | bytes accessed | tf_op | source)
XLA Modules:
  0.0 281.6 jit_solution(10589355332793551699)
XLA Ops:
  0.0 3.8 %collect_blocks.1 = (bf16[2,2,1152,128]{3,2,1,0:T(8,128)(2,1)}, f32[36,8,128]{2,1,0:T(8,128)}, f32[4,8,640]{2,1,0:T(8,128)}) custom-call(s32[2,2]{1,0:T(2,128)} %cols.1, s32[2,8]{1,0:T(2,128)} %offs.1, bf16[2048,256]{1,0:T(8,128)(2,1)} %keys_hbm.1, bf16[2048,256]{1,0:T(8,128)(2,1)} %values_hbm.1), custom_call_target="tpu_custom_call" | custom-call | tf_op jit(solution)/shard_map/collect_blocks/pallas_call | solution.py:227
  3.8 16.9 %exchange_and_attention.1 = (f32[128,4096]{1,0:T(8,128)}, bf16[128,4096]{1,0:T(8,128)(2,1)}, bf16[3,4,2,32,128]{4,3,2,1,0:T(8,128)(2,1)}) custom-call(bf16[2,2,1152,128]{3,2,1,0:T(8,128)(2,1)} %get-tuple-element.13.con_hbm, f32[36,8,128]{2,1,0:T(8,128)} %get-tuple-element.14.near_hbm, s32[8,128]{1,0:T(8,128)} %bitcast.10, f32[8,128]{1,0:T(8,128)} %bitcast.11, ...), custom_call_target="tpu_custom_call" | custom-call | tf_op jit(solution)/shard_map/exchange_and_attention/pallas_call | solution.py:442
  20.7 131.3 %dispatch.1 = (bf16[1280,768]{1,0:T(8,128)(2,1)}, f32[3,8,2,32,128]{4,3,2,1,0:T(8,128)}) custom-call(bf16[128,4096]{1,0:T(8,128)(2,1)} %get-tuple-element.16.normed_hbm, bf16[3,4,2,32,128]{4,3,2,1,0:T(8,128)(2,1)} %get-tuple-element.17.table_hbm, bf16[4096,768]{1,0:T(8,128)(2,1)} %bitcast.7, bf16[4096,768]{1,0:T(8,128)(2,1)} %bitcast.8), custom_call_target="tpu_custom_call" | custom-call | tf_op jit(solution)/shard_map/dispatch/pallas_call | solution.py:700
  152.0 127.3 %combine.1 = bf16[128,4096]{1,0:T(8,128)(2,1)} custom-call(bf16[1280,768]{1,0:T(8,128)(2,1)} %get-tuple-element.18.act_hbm, f32[3,8,2,32,128]{4,3,2,1,0:T(8,128)} %get-tuple-element.19.tables_hbm, bf16[768,4096]{1,0:T(8,128)(2,1)} %bitcast.6, f32[128,4096]{1,0:T(8,128)} %get-tuple-element.20.hidden_hbm), custom_call_target="tpu_custom_call" | custom-call | tf_op jit(solution)/shard_map/combine/pallas_call | solution.py:897
  279.4 2.3 copy.16

commit v5 on v4

--- a/solution.py
+++ b/solution.py
@@ -273,14 +273,6 @@
     for load in loads[:2]:
         load.wait()
 
-    first = pltpu.make_async_remote_copy(
-        src_ref=con.at[1 - c], dst_ref=sib, send_sem=ssem.at[0], recv_sem=rsem.at[0],
-        device_id=twin, device_id_type=MESH,
-    )
-    first.start()
-    first.wait()
-    chip[...] = con[c] + sib[...]
-
     verts = VERT * BLOCK
 
     def whole(h):
@@ -296,14 +288,25 @@
             device_id=across[h], device_id_type=MESH,
         )
 
-    @pl.when(xl == 0)
-    def _():
-        for h in range(HEADS_KV):
+    firsts = [
+        pltpu.make_async_remote_copy(
+            src_ref=con.at[1 - c, h], dst_ref=sib.at[h], send_sem=ssem.at[5 * h], recv_sem=rsem.at[5 * h],
+            device_id=twin, device_id_type=MESH,
+        )
+        for h in range(HEADS_KV)
+    ]
+    for first in firsts:
+        first.start()
+    for h in range(HEADS_KV):
+        firsts[h].wait()
+        chip[h] = con[c, h] + sib[h]
+
+        @pl.when(xl == 0)
+        def _():
             whole(h).start()
 
-    @pl.when(xl == 1)
-    def _():
-        for h in range(HEADS_KV):
+        @pl.when(xl == 1)
+        def _():
             vertical(h).start()
 
     for load in loads[2:]:
@@ -452,8 +455,8 @@
         + [
             pltpu.SemaphoreType.DMA((len(args),)),
             pltpu.SemaphoreType.DMA((6,)),
-            pltpu.SemaphoreType.DMA((5,)),
-            pltpu.SemaphoreType.DMA((5,)),
+            pltpu.SemaphoreType.DMA((6,)),
+            pltpu.SemaphoreType.DMA((6,)),
         ],
         compiler_params=pltpu.CompilerParams(
             collective_id=1, has_side_effects=True, vmem_limit_bytes=60 * 2**20
@@ -514,14 +517,21 @@
             device_id=turned_device(t, dev), device_id_type=MESH,
         )
 
-    for t in range(TYPES):
+    def send_tables(t):
         here = turned(t)
         me = here[2] * 2 + here[3]
         for n, o in enumerate(COLUMN):
             table_copy(n, t, to_column(o, here), me).start()
         tables[t, me] = table[t, here[2]]
 
-    def send_columns(j, carry):
+    def await_tables(t):
+        here = turned(t)
+        for n, o in enumerate(COLUMN):
+            dev = from_column(o, here)
+            table_copy(n, t, dev, dev[2] * 2 + dev[3]).wait()
+        tables_out[t] = tables[t].astype(F32)
+
+    def send_columns(j):
         t = j % 3
         here = turned(t)
         me = here[2] * 2 + here[3]
@@ -529,16 +539,18 @@
             column_copy(n, j, t, to_column(o, here), me).start()
         start = pl.multiple_of(here[3] * HALF + j * PIECE, PIECE)
         x_all[j, pl.ds(pl.multiple_of(me * TOK, TOK), TOK), :] = normed[:, pl.ds(start, PIECE)]
+
+    send_tables(0)
+    send_columns(0)
+    for t in range(1, TYPES):
+        send_tables(t)
+
+    def send_rest(j, carry):
+        send_columns(j)
         return carry
 
-    lax.fori_loop(0, PIECES, send_columns, 0)
-
-    for t in range(TYPES):
-        here = turned(t)
-        for n, o in enumerate(COLUMN):
-            dev = from_column(o, here)
-            table_copy(n, t, dev, dev[2] * 2 + dev[3]).wait()
-    tables_out[...] = tables[...].astype(F32)
+    lax.fori_loop(1, PIECES, send_rest, 0)
+    await_tables(0)
 
     block, place = table_rows()
 
@@ -658,6 +670,8 @@
 
         @pl.when(j == 0)
         def _():
+            for t in range(1, TYPES):
+                await_tables(t)
             acc[...] = jnp.zeros_like(acc)
             swap[...] = swap_matrix()
 

time: 284 us -> 283 us (level)
  no operation moved by 1% of the time
where the time goes in v5:
time: 283 us; the launch traced here: 281 us
  Pallas kernels  279 us (99%)
    pallas_call x1, Pallas kernels, dispatch(): pl.pallas_call(dispatch_kernel, name='dispatch', out_shape=[jax.ShapeDtyp...  131 us
    pallas_call x1, Pallas kernels, combine(): pl.pallas_call(combine_kernel, name='combine', out_shape=jax.ShapeDtypeSt...  127 us
    pallas_call x1, Pallas kernels, front(): pl.pallas_call(front_kernel, name='exchange_and_attention', out_shape=[ja...  16.8 us

profile of v5, /device:TPU:5, one launch (start us, length us, event | category | flops | bytes accessed | tf_op | source)
XLA Modules:
  0.0 281.2 jit_solution(4924473971240616015)
XLA Ops:
  0.0 3.8 %collect_blocks.1 = (bf16[2,2,1152,128]{3,2,1,0:T(8,128)(2,1)}, f32[36,8,128]{2,1,0:T(8,128)}, f32[4,8,640]{2,1,0:T(8,128)}) custom-call(s32[2,2]{1,0:T(2,128)} %cols.1, s32[2,8]{1,0:T(2,128)} %offs.1, bf16[2048,256]{1,0:T(8,128)(2,1)} %keys_hbm.1, bf16[2048,256]{1,0:T(8,128)(2,1)} %values_hbm.1), custom_call_target="tpu_custom_call" | custom-call | tf_op jit(solution)/shard_map/collect_blocks/pallas_call | solution.py:227
  3.8 16.8 %exchange_and_attention.1 = (f32[128,4096]{1,0:T(8,128)}, bf16[128,4096]{1,0:T(8,128)(2,1)}, bf16[3,4,2,32,128]{4,3,2,1,0:T(8,128)(2,1)}) custom-call(bf16[2,2,1152,128]{3,2,1,0:T(8,128)(2,1)} %get-tuple-element.13.con_hbm, f32[36,8,128]{2,1,0:T(8,128)} %get-tuple-element.14.near_hbm, s32[8,128]{1,0:T(8,128)} %bitcast.10, f32[8,128]{1,0:T(8,128)} %bitcast.11, ...), custom_call_target="tpu_custom_call" | custom-call | tf_op jit(solution)/shard_map/exchange_and_attention/pallas_call | solution.py:445
  20.7 130.9 %dispatch.1 = (bf16[1280,768]{1,0:T(8,128)(2,1)}, f32[3,8,2,32,128]{4,3,2,1,0:T(8,128)}) custom-call(bf16[128,4096]{1,0:T(8,128)(2,1)} %get-tuple-element.16.normed_hbm, bf16[3,4,2,32,128]{4,3,2,1,0:T(8,128)(2,1)} %get-tuple-element.17.table_hbm, bf16[4096,768]{1,0:T(8,128)(2,1)} %bitcast.7, bf16[4096,768]{1,0:T(8,128)(2,1)} %bitcast.8), custom_call_target="tpu_custom_call" | custom-call | tf_op jit(solution)/shard_map/dispatch/pallas_call | solution.py:714
  151.6 127.3 %combine.1 = bf16[128,4096]{1,0:T(8,128)(2,1)} custom-call(bf16[1280,768]{1,0:T(8,128)(2,1)} %get-tuple-element.18.act_hbm, f32[3,8,2,32,128]{4,3,2,1,0:T(8,128)} %get-tuple-element.19.tables_hbm, bf16[768,4096]{1,0:T(8,128)(2,1)} %bitcast.6, f32[128,4096]{1,0:T(8,128)} %get-tuple-element.20.hidden_hbm), custom_call_target="tpu_custom_call" | custom-call | tf_op jit(solution)/shard_map/combine/pallas_call | solution.py:911
  278.9 2.3 copy.16
